TPU v7x, 128 devices: a whole 4x4x4 slice. The times are simulated.
128 devices in a mesh: dp: 16 (over y, x_lo, core), tp: 8 (over x_hi, z).
Axes of the slice: x: 4 (x_hi: 2, x_lo: 2; x = x_hi * 2 + x_lo), y: 4, z: 4, core: 2. Of those that a mesh axis runs over, the one named last changes fastest.
Arguments:
- queries: bfloat16 [8192, 8192], P('dp', 'tp'), may hold values from -72 to 72
- kv_pool: bfloat16 [256, 128, 2048], P('dp', None, 'tp'), may hold values from -12 to 12
- span_start: int32 [16], P('dp'), may hold values from 0 to 12, as said below
- page_table: int32 [16, 16], P('dp'), may hold values from 0 to 15, each once within a row
- fire_slope: float32 [32], replicated, may hold values from -6 to 6
- fire_shift: float32 [32], replicated, may hold values from -1 to 1
- fire_mix: float32 [32, 64], P(None, 'tp'), may hold values from -3 to 3
- out_weight: bfloat16 [8192, 8192], P('tp'), may hold values from -0.0625 to 0.0625
Outputs:
- mixed: bfloat16 [8192, 8192], P('dp', 'tp')
Inputs may be any that keep to these rules, and one draw needn't show every extreme that they name: Each request's span ends at page span_start + 4 at the latest on page 16, and one request reaches it. `page_table`: each row lists every pool slot of its request once.
All inputs are finite; a program needn't handle non-finite values.
Results may differ from a plain program's by a relative error of at most 0.019.
Values may be sent and summed in bfloat16 or wider, within the bound.
No kernel may reach another device: no remote copies, remote signals or barrier semaphores. Data moves between devices by JAX's collectives and lax.ppermute only.
A program may use at most 128 MiB of HBM per device.

v0:
```python
import functools
import math

import jax
import jax.numpy as jnp
from jax import lax
from jax.experimental import pallas as pl
from jax.experimental.pallas import tpu as pltpu
from jax.sharding import PartitionSpec as P

HEAD_DIM = 128
PAGE = 128
HEADS = 8
HIDDEN = 32
CHUNK = 128
KEYS = 256
GROUP = 32
WIDE = HEADS * CHUNK
COLUMNS = 1024
TILES = 2048 // KEYS
THRESHOLD = 32
NEG = -1e30
SCALE = HEAD_DIM**-0.5
TO_EXP2 = SCALE * math.log2(math.e)
MIB = 1 << 20


def column_blocks():
    me = lax.axis_index("tp")
    core = lax.rem(lax.axis_index("dp"), 2)
    hi, z = me // 4, lax.rem(me, 4)
    flip, mirror = z + 1 - 2 * lax.rem(z, 2), 3 - z
    first = jnp.where(core == 0, flip, mirror)
    second = jnp.where(core == 0, mirror, flip)
    both = 3 - first
    both = jnp.where(core == 0, 3 - flip, mirror + 1 - 2 * lax.rem(mirror, 2))
    own, other = hi * 4, (1 - hi) * 4
    return [
        own + first, own + both, other + first, other + both,
        other + z, other + second, own + z, own + second,
    ]


def attention(chunk, params, q_ref, kv_ref, units_ref, qt, acc, peak, mass, scores, probs, scale, xs, lines, bits, kinks, att):
    start_ref, table_ref, fire_ref = params
    row0 = (start_ref[0] + chunk) * PAGE
    for h in range(HEADS):
        qt[:, h * 128 : (h + 1) * 128] = q_ref[:, h * 128 : (h + 1) * 128].T
    acc[...] = jnp.zeros_like(acc)
    mass[...] = jnp.zeros_like(mass)
    peak[...] = jnp.full_like(peak, NEG)
    probs[1][...] = jnp.zeros_like(probs[1])
    scale[1][...] = jnp.zeros_like(scale[1])
    rows = row0 + lax.broadcasted_iota(jnp.int32, (1, CHUNK), 1)
    rec = 1.0 / jnp.log(1.0 + jnp.maximum(rows, THRESHOLD).astype(jnp.float32))
    ahead = lax.broadcasted_iota(jnp.int32, (KEYS, CHUNK), 1) - lax.broadcasted_iota(
        jnp.int32, (KEYS, CHUNK), 0
    )
    pages = KEYS // PAGE
    tiles = (start_ref[0] + chunk + pages) // pages

    def slots(b):
        return [table_ref[0, jnp.minimum(b * pages + n, 15)] for n in range(pages)]

    gaps = row0 - KEYS * lax.broadcasted_iota(jnp.int32, (TILES, 128), 0)
    least_log = jnp.log(1.0 + jnp.maximum(gaps - (KEYS - 1), 0).astype(jnp.float32))
    most_log = jnp.log(1.0 + jnp.maximum(gaps + (CHUNK - 1), 0).astype(jnp.float32))
    low = least_log * (jnp.min(rec, axis=1, keepdims=True) * (1 - 1e-5))
    high = most_log * (jnp.max(rec, axis=1, keepdims=True) * (1 + 1e-5))
    slope, shift, mix = units_ref[0:1], units_ref[1:2], units_ref[8:16]
    at_low, at_high = slope * low + shift, slope * high + shift
    least, most = jnp.minimum(at_low, at_high), jnp.maximum(at_low, at_high)
    unit = lax.broadcasted_iota(jnp.int32, (TILES, 128), 1)
    weight = jnp.left_shift(1, unit & 15).astype(jnp.float32)
    weight = jnp.where((least < 0) & (most > 0), weight, 0.0)
    weights = jnp.where(unit < 16, weight, 0.0), jnp.where(unit < 16, 0.0, weight)
    shift_on, slope_on = jnp.where(least >= 0, shift, 0.0), jnp.where(least >= 0, slope, 0.0)
    for b in range(TILES):
        for n, on in enumerate((shift_on, slope_on)):
            line = jnp.sum(mix * on[b : b + 1], axis=1, keepdims=True)
            lines[b, n] = jnp.broadcast_to(line, (HEADS, CHUNK))
            bits[b, n] = jnp.sum(weights[n][b : b + 1]).astype(jnp.int32)

    def score(b, slot):
        k = jnp.concatenate([kv_ref[s, :, :128] for s in slots(b)], axis=0)
        for g in range(HEADS // 2):
            columns = slice(g * 256, (g + 1) * 256)
            scores[slot][:, columns] = jnp.dot(k, qt[:, columns], preferred_element_type=jnp.float32)
        gap = row0 - b * KEYS
        xs[slot][...] = jnp.log(1.0 + jnp.maximum(ahead + gap, 0).astype(jnp.float32)) * rec

    def mend(b, slot):
        gap = row0 - b * KEYS
        halves = bits[jnp.minimum(b, TILES - 1), 0], bits[jnp.minimum(b, TILES - 1), 1]

        @pl.when((halves[0] + halves[1] > 0) | (gap < KEYS - 1))
        def _():
            bent = jnp.int32(0)
            for f in range(HIDDEN):
                kinks[bent] = f
                bent = bent + (lax.shift_right_logical(halves[f // 16], f % 16) & 1)
            kinks[bent] = HIDDEN

            def group(n, carry):
                at = pl.ds(pl.multiple_of(n * GROUP, GROUP), GROUP)
                x = xs[slot][at, :]

                def unit(e, terms):
                    f, g = kinks[2 * e], kinks[2 * e + 1]
                    one = jnp.maximum(fire_ref[0, f] * x + fire_ref[1, f], 0.0)
                    two = jnp.maximum(fire_ref[0, g] * x + fire_ref[1, g], 0.0)
                    return tuple(
                        t + (fire_ref[8 + h, f] * one + fire_ref[8 + h, g] * two)
                        for h, t in enumerate(terms)
                    )

                terms = tuple(scores[slot][at, h * 128 : (h + 1) * 128] for h in range(HEADS))
                terms = lax.fori_loop(0, (bent + 1) // 2, unit, terms)
                seen = ahead[:GROUP] + (gap - n * GROUP) >= 0
                for h in range(HEADS):
                    scores[slot][at, h * 128 : (h + 1) * 128] = jnp.where(seen, terms[h], NEG)
                return carry

            lax.fori_loop(0, KEYS // GROUP, group, 0)

    def weigh(b, slot):
        b = jnp.minimum(b, TILES - 1)
        for h in range(HEADS):
            columns = slice(h * 128, (h + 1) * 128)
            flat = lines[b, 0, h : h + 1]
            t = scores[slot][:, columns] + lines[b, 1, h : h + 1] * xs[slot][...]
            before = peak[h : h + 1]
            after = jnp.maximum(before, jnp.max(t, axis=0, keepdims=True) + flat)
            factor = jnp.exp2((before - after) * TO_EXP2)
            p = jnp.exp2((t - (after - flat)) * TO_EXP2)
            mass[h] = mass[h] * factor + jnp.sum(p.reshape(KEYS // 8, 8, CHUNK), axis=0)
            peak[h : h + 1] = after
            scale[slot][:, columns] = factor
            probs[slot][:, columns] = p.astype(jnp.bfloat16)

    def gather(b, slot):
        vt = jnp.concatenate([kv_ref[s, :, 128:].T for s in slots(b)], axis=1)
        for g in range(HEADS // 2):
            columns = slice(g * 256, (g + 1) * 256)
            update = jnp.dot(vt, probs[slot][:, columns], preferred_element_type=jnp.float32)
            acc[:, columns] = acc[:, columns] * scale[slot][:, columns] + update

    def step(b, slot):
        mend(b, slot)
        score(b + 1, 1 - slot)
        gather(jnp.maximum(b - 1, 0), 1 - slot)
        weigh(b, slot)

    def tile(b, carry):
        for slot in range(2):
            pl.when(b % 2 == slot)(functools.partial(step, b, slot))
        return carry

    score(0, 0)
    lax.fori_loop(0, tiles, tile, 0)
    for slot in range(2):
        pl.when(tiles % 2 != slot)(functools.partial(gather, tiles - 1, slot))
    for h in range(HEADS):
        columns = slice(h * 128, (h + 1) * 128)
        total = jnp.sum(mass[h], axis=0, keepdims=True)
        att[:, columns] = (acc[:, columns] / total).T.astype(jnp.bfloat16)


def kernel(chunk, *refs):
    params, (units_ref, q_ref, kv_ref, w_ref) = refs[:3], refs[3:7]
    outs, scratch = refs[-23:-20], refs[-20:]
    (
        qt, acc, peak, mass, s0, s1, p0, p1, f0, f1, x0, x1, lines, bits, kinks, att,
        wbuf, stage, fetched, stored,
    ) = scratch
    blocks = column_blocks()

    def fetch(n):
        columns = pl.ds(pl.multiple_of(blocks[n] * COLUMNS, COLUMNS), COLUMNS)
        return pltpu.make_async_copy(w_ref.at[:, columns], wbuf.at[n], fetched.at[n])

    for n in range(8):
        fetch(n).start()
    attention(
        chunk, params, q_ref, kv_ref, units_ref, qt, acc, peak, mass,
        (s0, s1), (p0, p1), (f0, f1), (x0, x1), lines, bits, kinks, att,
    )
    for n in range(8):
        fetch(n).wait()

    def block(n, carry):
        stage[n] = jnp.dot(att[...], wbuf[n], preferred_element_type=jnp.float32).astype(jnp.bfloat16)
        return carry

    copies = []
    for n, (ref, first, count) in enumerate(zip(outs, (0, 4, 6), (4, 2, 2))):
        lax.fori_loop(first, first + count, block, 0)
        copies.append(pltpu.make_async_copy(stage.at[first : first + count], ref, stored.at[n]))
        copies[-1].start()
    for copy in copies:
        copy.wait()


def partial_sums(chunk, start, table, units, queries, kv, w, after=()):
    smem = pl.BlockSpec(memory_space=pltpu.SMEM)
    return pl.pallas_call(
        functools.partial(kernel, chunk),
        grid=(1,),
        in_specs=[smem] * 3
        + [
            pl.BlockSpec((16, 128), lambda i: (0, 0)),
            pl.BlockSpec((CHUNK, HEADS * 128), lambda i: (chunk, 0)),
            pl.BlockSpec((16, PAGE, 256), lambda i: (0, 0, 0)),
        ]
        + [pl.BlockSpec(memory_space=pl.ANY)] * (1 + len(after)),
        out_specs=[pl.BlockSpec(memory_space=pl.ANY)] * 3,
        out_shape=[
            jax.ShapeDtypeStruct((n, CHUNK, COLUMNS), jnp.bfloat16) for n in (4, 2, 2)
        ],
        scratch_shapes=[
            pltpu.VMEM((128, WIDE), jnp.bfloat16),
            pltpu.VMEM((128, WIDE), jnp.float32),
            pltpu.VMEM((HEADS, CHUNK), jnp.float32),
            pltpu.VMEM((HEADS, 8, CHUNK), jnp.float32),
        ]
        + [pltpu.VMEM((KEYS, WIDE), jnp.float32)] * 2
        + [pltpu.VMEM((KEYS, WIDE), jnp.bfloat16)] * 2
        + [pltpu.VMEM((1, WIDE), jnp.float32)] * 2
        + [pltpu.VMEM((KEYS, CHUNK), jnp.float32)] * 2
        + [
            pltpu.VMEM((TILES, 2, HEADS, CHUNK), jnp.float32),
            pltpu.SMEM((TILES, 2), jnp.int32),
            pltpu.SMEM((HIDDEN + 1,), jnp.int32),
            pltpu.VMEM((CHUNK, HEADS * 128), jnp.bfloat16),
            pltpu.VMEM((8, HEADS * 128, COLUMNS), jnp.bfloat16),
            pltpu.VMEM((8, CHUNK, COLUMNS), jnp.bfloat16),
            pltpu.SemaphoreType.DMA((8,)),
            pltpu.SemaphoreType.DMA((3,)),
        ],
        compiler_params=pltpu.CompilerParams(vmem_limit_bytes=60 * MIB),
        cost_estimate=pl.CostEstimate(
            flops=12 * 10**9, bytes_accessed=20 * MIB, transcendentals=CHUNK * 2048 * 8
        ),
        name=f"chunk{chunk}",
    )(start, table, units, units, queries, kv, w, *after)


def swap(x, step):
    pairs = []
    for dp in range(16):
        for hi in range(2):
            for z in range(4):
                if step == 1:
                    to = (1 - hi) * 4 + z
                else:
                    to = hi * 4 + ((z ^ 1) if (dp + step // 2) % 2 == 0 else 3 - z)
                pairs.append((dp * 8 + hi * 4 + z, dp * 8 + to))
    return lax.ppermute(x, ("dp", "tp"), pairs)


def shards(queries, kv_pool, span_start, page_table, fire_slope, fire_shift, fire_mix, out_weight):
    units = jnp.concatenate(
        [fire_slope[None], fire_shift[None], jnp.zeros((6, HIDDEN), jnp.float32), fire_mix.T / SCALE]
    )
    units = jnp.pad(units, ((0, 0), (0, 128 - HIDDEN)))
    f32, bf16 = jnp.float32, jnp.bfloat16
    chunks = queries.shape[0] // CHUNK
    mine, got, got_x, part, outs = ([None] * chunks for _ in range(5))

    def along_x(c):
        got[c] = swap(mine[c][0], 0)
        return (mine[c][1].astype(f32) + got[c][2:].astype(f32)).astype(bf16)

    def along_z(c, crossed):
        got_x[c] = swap(crossed, 1)
        part[c] = [
            mine[c][2][n].astype(f32) + got[c][n].astype(f32) + got_x[c][n].astype(f32)
            for n in range(2)
        ]
        return part[c][1].astype(bf16)

    crossed, last = [None] * chunks, [None] * chunks
    for c in range(chunks):
        after = []
        if c >= 1:
            after.append(mine[c - 1][0])
        if c >= 2:
            crossed[c - 2] = along_x(c - 2)
            after.append(crossed[c - 2])
        if c >= 3:
            last[c - 3] = along_z(c - 3, crossed[c - 3])
            after.append(last[c - 3])
        mine[c] = partial_sums(c, span_start, page_table, units, queries, kv_pool, out_weight, after)
    for c in range(chunks):
        if crossed[c] is None:
            crossed[c] = along_x(c)
        if last[c] is None:
            last[c] = along_z(c, crossed[c])
        outs[c] = (part[c][0] + swap(last[c], 2).astype(f32)).astype(bf16)
    return jnp.concatenate(outs, axis=0)


def solution(mesh):
    in_specs = (
        P("dp", "tp"),
        P("dp", None, "tp"),
        P("dp"),
        P("dp", None),
        P(),
        P(),
        P(None, "tp"),
        P("tp", None),
    )
    out_specs = P("dp", "tp")
    return jax.shard_map(shards, mesh=mesh, in_specs=in_specs, out_specs=out_specs, check_vma=False)
```

profile of v0, /device:TPU:18, one launch (start us, length us, event | category | flops | bytes accessed | tf_op | source)
XLA Modules:
  0.0 122.4 jit_solution(1631785675598574524)
XLA Ops:
  0.7 0.7 multiply_bitcast_fusion
  1.4 0.7 pad_maximum_fusion.1
  2.2 0.6 pad.4.refs_2_.refs_3_
  2.8 16.7 %chunk0.1 = (bf16[4,128,1024]{2,1,0:T(8,128)(2,1)}, bf16[2,128,1024]{2,1,0:T(8,128)(2,1)}, bf16[2,128,1024]{2,1,0:T(8,128)(2,1)}) custom-call(s32[1]{0:T(128)S(6)} %copy.9.refs_0_, s32[1,16]{1,0:T(1,128)} %refs_1_.7, f32[16,128]{1,0:T(8,128)} %pad.4.refs_2_.refs_3_, f32[16,128]{1,0:T(8,128)} %pad.4.refs_2_.refs_3_, bf16[512,1024]{1,0:T(8,128)(2,1)} %refs_4_.7, ...), custom_call_target="tpu_custom_call" | custom-call | flops 12000000000 | bytes 20971520 | tf_op jit(solution)/shard_map/chunk0/pallas_call | solution.py:206
  19.5 2.0 %collective-permute-start = (bf16[4,128,1024]{2,1,0:T(8,128)(2,1)}, bf16[4,128,1024]{2,1,0:T(8,128)(2,1)S(1)}, u32[]{:S(2)}, u32[]{:S(2)}) collective-permute-start(bf16[4,128,1024]{2,1,0:T(8,128)(2,1)} %get-tuple-element.18.refs_7_), channel_id=1, source_target_pairs={{0,1},{1,0},{2,3},{3,2},{4,5},{5,4},{6,7},{7,6},{8,11},{9,10},{10,... | collective-permute-start | bytes 3145736 | tf_op jit(solution)/shard_map/ppermute | solution.py:258
  21.5 15.2 %chunk1.1 = (bf16[4,128,1024]{2,1,0:T(8,128)(2,1)}, bf16[2,128,1024]{2,1,0:T(8,128)(2,1)}, bf16[2,128,1024]{2,1,0:T(8,128)(2,1)}) custom-call(s32[1]{0:T(128)S(6)} %copy.9.refs_0_, s32[1,16]{1,0:T(1,128)} %refs_1_.7, f32[16,128]{1,0:T(8,128)} %pad.4.refs_2_.refs_3_, f32[16,128]{1,0:T(8,128)} %pad.4.refs_2_.refs_3_, bf16[512,1024]{1,0:T(8,128)(2,1)} %refs_4_.7, ...), custom_call_target="tpu_custom_call" | custom-call | flops 12000000000 | bytes 20971520 | tf_op jit(solution)/shard_map/chunk1/pallas_call | solution.py:206
  36.7 0.2 collective-permute-start.3
  36.9 1.0 add_convert_fusion.3.refs_8_
  37.9 2.1 %collective-permute-start.1 = (bf16[2,128,1024]{2,1,0:T(8,128)(2,1)}, bf16[2,128,1024]{2,1,0:T(8,128)(2,1)}, u32[]{:S(2)}, u32[]{:S(2)}) collective-permute-start(bf16[2,128,1024]{2,1,0:T(8,128)(2,1)} %add_convert_fusion.3.refs_8_), channel_id=1, source_target_pairs={{0,4},{1,5},{2,6},{3,7},{4,0},{5,1},{6,2},{7,3},{8,12},{9,13},{10,... | collective-permute-start | bytes 1572872 | tf_op jit(solution)/shard_map/ppermute | solution.py:258
  40.0 17.9 %chunk2.1 = (bf16[4,128,1024]{2,1,0:T(8,128)(2,1)}, bf16[2,128,1024]{2,1,0:T(8,128)(2,1)}, bf16[2,128,1024]{2,1,0:T(8,128)(2,1)}) custom-call(s32[1]{0:T(128)S(6)} %copy.9.refs_0_, s32[1,16]{1,0:T(1,128)} %refs_1_.7, f32[16,128]{1,0:T(8,128)} %pad.4.refs_2_.refs_3_, f32[16,128]{1,0:T(8,128)} %pad.4.refs_2_.refs_3_, bf16[512,1024]{1,0:T(8,128)(2,1)} %refs_4_.7, ...), custom_call_target="tpu_custom_call" | custom-call | flops 12000000000 | bytes 20971520 | tf_op jit(solution)/shard_map/chunk2/pallas_call | solution.py:206
  58.0 2.2 %collective-permute-start.6 = (bf16[4,128,1024]{2,1,0:T(8,128)(2,1)}, bf16[4,128,1024]{2,1,0:T(8,128)(2,1)S(1)}, u32[]{:S(2)}, u32[]{:S(2)}) collective-permute-start(bf16[4,128,1024]{2,1,0:T(8,128)(2,1)} %get-tuple-element.24.refs_7_), channel_id=1, source_target_pairs={{0,1},{1,0},{2,3},{3,2},{4,5},{5,4},{6,7},{7,6},{8,11},{9,10},{10,... | collective-permute-start | bytes 3145736 | tf_op jit(solution)/shard_map/ppermute | solution.py:258
  60.2 1.0 add_convert_fusion.2.refs_8_
  61.1 1.9 %fusion.4.refs_9_ = bf16[128,1024]{1,0:T(8,128)(2,1)} fusion(bf16[2,128,1024]{2,1,0:T(8,128)(2,1)} %collective-permute-done.1, bf16[4,128,1024]{2,1,0:T(8,128)(2,1)S(1)} %collective-permute-done, bf16[2,128,1024]{2,1,0:T(8,128)(2,1)} %get-tuple-element.17), kind=kLoop, calls=%fused_computation.17 | loop fusion | flops 786432 | bytes 1048576 | tf_op jit(solution)/shard_map/convert_element_type | solution.py:280
  63.0 15.7 %chunk3.1 = (bf16[4,128,1024]{2,1,0:T(8,128)(2,1)}, bf16[2,128,1024]{2,1,0:T(8,128)(2,1)}, bf16[2,128,1024]{2,1,0:T(8,128)(2,1)}) custom-call(s32[1]{0:T(128)S(6)} %copy.9.refs_0_, s32[1,16]{1,0:T(1,128)} %refs_1_.7, f32[16,128]{1,0:T(8,128)} %pad.4.refs_2_.refs_3_, f32[16,128]{1,0:T(8,128)} %pad.4.refs_2_.refs_3_, bf16[512,1024]{1,0:T(8,128)(2,1)} %refs_4_.7, ...), custom_call_target="tpu_custom_call" | custom-call | flops 12000000000 | bytes 20971520 | tf_op jit(solution)/shard_map/chunk3/pallas_call | solution.py:206
  78.7 0.2 collective-permute-start.9
  78.9 1.4 %collective-permute-start.4 = (bf16[2,128,1024]{2,1,0:T(8,128)(2,1)S(1)}, bf16[2,128,1024]{2,1,0:T(8,128)(2,1)S(1)}, u32[]{:S(2)}, u32[]{:S(2)}) collective-permute-start(bf16[2,128,1024]{2,1,0:T(8,128)(2,1)S(1)} %copy-done), channel_id=1, source_target_pairs={{0,4},{1,5},{2,6},{3,7},{4,0},{5,1},{6,2},{7,3},{8,12},{9,13},{10,... | collective-permute-start | bytes 1572872 | tf_op jit(solution)/shard_map/ppermute | solution.py:258
  80.3 4.0 %collective-permute-start.2 = (bf16[128,1024]{1,0:T(8,128)(2,1)S(1)}, bf16[128,1024]{1,0:T(8,128)(2,1)S(1)}, u32[]{:S(2)}, u32[]{:S(2)}) collective-permute-start(bf16[128,1024]{1,0:T(8,128)(2,1)S(1)} %copy-done.7), channel_id=1, source_target_pairs={{0,3},{1,2},{2,1},{3,0},{4,7},{5,6},{6,5},{7,4},{8,9},{9,8},{10,11... | collective-permute-start | bytes 786440 | tf_op jit(solution)/shard_map/ppermute | solution.py:258
  84.4 1.3 %add_convert_fusion.1 = bf16[2,128,1024]{2,1,0:T(8,128)(2,1)S(1)} fusion(bf16[2,128,1024]{2,1,0:T(8,128)(2,1)} %get-tuple-element.25, bf16[4,128,1024]{2,1,0:T(8,128)(2,1)S(1)} %collective-permute-done.6), kind=kLoop, calls=%fused_computation.2 | loop fusion | flops 1048576 | bytes 1572864 | tf_op jit(solution)/shard_map/convert_element_type | solution.py:272
  85.7 2.2 %collective-permute-start.7 = (bf16[2,128,1024]{2,1,0:T(8,128)(2,1)S(1)}, bf16[2,128,1024]{2,1,0:T(8,128)(2,1)S(1)}, u32[]{:S(2)}, u32[]{:S(2)}) collective-permute-start(bf16[2,128,1024]{2,1,0:T(8,128)(2,1)S(1)} %add_convert_fusion.1), channel_id=1, source_target_pairs={{0,4},{1,5},{2,6},{3,7},{4,0},{5,1},{6,2},{7,3},{8,12},{9,13},{10,... | collective-permute-start | bytes 1572872 | tf_op jit(solution)/shard_map/ppermute | solution.py:258
  87.9 11.5 %collective-permute-done.9 = bf16[4,128,1024]{2,1,0:T(8,128)(2,1)S(1)} collective-permute-done((bf16[4,128,1024]{2,1,0:T(8,128)(2,1)}, bf16[4,128,1024]{2,1,0:T(8,128)(2,1)S(1)}, u32[]{:S(2)}, u32[]{:S(2)}) %collective-permute-start.9) | collective-permute-done | bytes 1048608 | tf_op jit(solution)/shard_map/ppermute | solution.py:258
  99.4 1.2 %add_convert_fusion = bf16[2,128,1024]{2,1,0:T(8,128)(2,1)S(1)} fusion(bf16[2,128,1024]{2,1,0:T(8,128)(2,1)} %get-tuple-element.28, bf16[4,128,1024]{2,1,0:T(8,128)(2,1)S(1)} %collective-permute-done.9), kind=kLoop, calls=%fused_computation.1 | loop fusion | flops 1048576 | bytes 1572864 | tf_op jit(solution)/shard_map/convert_element_type | solution.py:272
  100.7 1.5 %collective-permute-start.10 = (bf16[2,128,1024]{2,1,0:T(8,128)(2,1)S(1)}, bf16[2,128,1024]{2,1,0:T(8,128)(2,1)S(1)}, u32[]{:S(2)}, u32[]{:S(2)}) collective-permute-start(bf16[2,128,1024]{2,1,0:T(8,128)(2,1)S(1)} %add_convert_fusion), channel_id=1, source_target_pairs={{0,4},{1,5},{2,6},{3,7},{4,0},{5,1},{6,2},{7,3},{8,12},{9,13},{10,... | collective-permute-start | bytes 1572872 | tf_op jit(solution)/shard_map/ppermute | solution.py:258
  102.2 0.1 fusion.5
  102.3 5.3 %collective-permute-start.5 = (bf16[128,1024]{1,0:T(8,128)(2,1)S(1)}, bf16[128,1024]{1,0:T(8,128)(2,1)S(1)}, u32[]{:S(2)}, u32[]{:S(2)}) collective-permute-start(bf16[128,1024]{1,0:T(8,128)(2,1)S(1)} %fusion.5), channel_id=1, source_target_pairs={{0,3},{1,2},{2,1},{3,0},{4,7},{5,6},{6,5},{7,4},{8,9},{9,8},{10,11... | collective-permute-start | bytes 786440 | tf_op jit(solution)/shard_map/ppermute | solution.py:258
  107.6 1.1 fusion.3
  109.0 2.4 %collective-permute-done.10 = bf16[2,128,1024]{2,1,0:T(8,128)(2,1)S(1)} collective-permute-done((bf16[2,128,1024]{2,1,0:T(8,128)(2,1)S(1)}, bf16[2,128,1024]{2,1,0:T(8,128)(2,1)S(1)}, u32[]{:S(2)}, u32[]{:S(2)}) %collective-permute-start.10) | collective-permute-done | bytes 524320 | tf_op jit(solution)/shard_map/ppermute | solution.py:258
  111.6 5.3 %collective-permute-start.11 = (bf16[128,1024]{1,0:T(8,128)(2,1)S(1)}, bf16[128,1024]{1,0:T(8,128)(2,1)S(1)}, u32[]{:S(2)}, u32[]{:S(2)}) collective-permute-start(bf16[128,1024]{1,0:T(8,128)(2,1)S(1)} %fusion.7), channel_id=1, source_target_pairs={{0,3},{1,2},{2,1},{3,0},{4,7},{5,6},{6,5},{7,4},{8,9},{9,8},{10,11... | collective-permute-start | bytes 786440 | tf_op jit(solution)/shard_map/ppermute | solution.py:258
  116.9 0.2 fusion.2
  117.1 0.2 fusion.1
  117.2 4.0 %collective-permute-done.11 = bf16[128,1024]{1,0:T(8,128)(2,1)S(1)} collective-permute-done((bf16[128,1024]{1,0:T(8,128)(2,1)S(1)}, bf16[128,1024]{1,0:T(8,128)(2,1)S(1)}, u32[]{:S(2)}, u32[]{:S(2)}) %collective-permute-start.11) | collective-permute-done | bytes 262176 | tf_op jit(solution)/shard_map/ppermute | solution.py:258
  121.2 0.2 fusion
  121.4 1.0 pad_maximum_fusion
  (30 shorter events, 0.5 us)
Async XLA Ops:
  19.5 17.4 %copy-start.2 = (bf16[2,128,1024]{2,1,0:T(8,128)(2,1)S(1)}, bf16[2,128,1024]{2,1,0:T(8,128)(2,1)}, u32[]{:S(2)}) copy-start(bf16[2,128,1024]{2,1,0:T(8,128)(2,1)} %get-tuple-element.19) | copy-start | bytes 1572868
  19.5 17.4 %collective-permute-start = (bf16[4,128,1024]{2,1,0:T(8,128)(2,1)}, bf16[4,128,1024]{2,1,0:T(8,128)(2,1)S(1)}, u32[]{:S(2)}, u32[]{:S(2)}) collective-permute-start(bf16[4,128,1024]{2,1,0:T(8,128)(2,1)} %get-tuple-element.18.refs_7_), channel_id=1, source_target_pairs={{0,1},{1,0},{2,3},{3,2},{4,5},{5,4},{6,7},{7,6},{8,11},{9,10},{10,... | collective-permute-start | bytes 3145736 | tf_op jit(solution)/shard_map/ppermute | solution.py:258
  36.7 23.4 %collective-permute-start.3 = (bf16[4,128,1024]{2,1,0:T(8,128)(2,1)}, bf16[4,128,1024]{2,1,0:T(8,128)(2,1)S(1)}, u32[]{:S(2)}, u32[]{:S(2)}) collective-permute-start(bf16[4,128,1024]{2,1,0:T(8,128)(2,1)} %get-tuple-element.21.refs_7_), channel_id=1, source_target_pairs={{0,1},{1,0},{2,3},{3,2},{4,5},{5,4},{6,7},{7,6},{8,11},{9,10},{10,... | collective-permute-start | bytes 3145736 | tf_op jit(solution)/shard_map/ppermute | solution.py:258
  37.9 22.2 %copy-start.1 = (bf16[2,128,1024]{2,1,0:T(8,128)(2,1)S(1)}, bf16[2,128,1024]{2,1,0:T(8,128)(2,1)}, u32[]{:S(2)}) copy-start(bf16[2,128,1024]{2,1,0:T(8,128)(2,1)} %get-tuple-element.22) | copy-start | bytes 1572868
  37.9 23.2 %collective-permute-start.1 = (bf16[2,128,1024]{2,1,0:T(8,128)(2,1)}, bf16[2,128,1024]{2,1,0:T(8,128)(2,1)}, u32[]{:S(2)}, u32[]{:S(2)}) collective-permute-start(bf16[2,128,1024]{2,1,0:T(8,128)(2,1)} %add_convert_fusion.3.refs_8_), channel_id=1, source_target_pairs={{0,4},{1,5},{2,6},{3,7},{4,0},{5,1},{6,2},{7,3},{8,12},{9,13},{10,... | collective-permute-start | bytes 1572872 | tf_op jit(solution)/shard_map/ppermute | solution.py:258
  58.0 26.4 %collective-permute-start.6 = (bf16[4,128,1024]{2,1,0:T(8,128)(2,1)}, bf16[4,128,1024]{2,1,0:T(8,128)(2,1)S(1)}, u32[]{:S(2)}, u32[]{:S(2)}) collective-permute-start(bf16[4,128,1024]{2,1,0:T(8,128)(2,1)} %get-tuple-element.24.refs_7_), channel_id=1, source_target_pairs={{0,1},{1,0},{2,3},{3,2},{4,5},{5,4},{6,7},{7,6},{8,11},{9,10},{10,... | collective-permute-start | bytes 3145736 | tf_op jit(solution)/shard_map/ppermute | solution.py:258
  63.0 15.9 %copy-start = (bf16[2,128,1024]{2,1,0:T(8,128)(2,1)S(1)}, bf16[2,128,1024]{2,1,0:T(8,128)(2,1)}, u32[]{:S(2)}) copy-start(bf16[2,128,1024]{2,1,0:T(8,128)(2,1)} %add_convert_fusion.2.refs_8_) | copy-start | bytes 1572868
  63.0 17.3 %copy-start.7 = (bf16[128,1024]{1,0:T(8,128)(2,1)S(1)}, bf16[128,1024]{1,0:T(8,128)(2,1)}, u32[]{:S(2)}) copy-start(bf16[128,1024]{1,0:T(8,128)(2,1)} %fusion.4.refs_9_) | copy-start | bytes 786436
  78.7 23.5 %copy-start.3 = (bf16[2,128,1024]{2,1,0:T(8,128)(2,1)S(1)}, bf16[2,128,1024]{2,1,0:T(8,128)(2,1)}, u32[]{:S(2)}) copy-start(bf16[2,128,1024]{2,1,0:T(8,128)(2,1)} %get-tuple-element.20) | copy-start | bytes 1572868
  78.7 20.7 %collective-permute-start.9 = (bf16[4,128,1024]{2,1,0:T(8,128)(2,1)}, bf16[4,128,1024]{2,1,0:T(8,128)(2,1)S(1)}, u32[]{:S(2)}, u32[]{:S(2)}) collective-permute-start(bf16[4,128,1024]{2,1,0:T(8,128)(2,1)} %get-tuple-element.27), channel_id=1, source_target_pairs={{0,1},{1,0},{2,3},{3,2},{4,5},{5,4},{6,7},{7,6},{8,11},{9,10},{10,... | collective-permute-start | bytes 3145736 | tf_op jit(solution)/shard_map/ppermute | solution.py:258
  78.9 23.3 %collective-permute-start.4 = (bf16[2,128,1024]{2,1,0:T(8,128)(2,1)S(1)}, bf16[2,128,1024]{2,1,0:T(8,128)(2,1)S(1)}, u32[]{:S(2)}, u32[]{:S(2)}) collective-permute-start(bf16[2,128,1024]{2,1,0:T(8,128)(2,1)S(1)} %copy-done), channel_id=1, source_target_pairs={{0,4},{1,5},{2,6},{3,7},{4,0},{5,1},{6,2},{7,3},{8,12},{9,13},{10,... | collective-permute-start | bytes 1572872 | tf_op jit(solution)/shard_map/ppermute | solution.py:258
  80.3 27.3 %collective-permute-start.2 = (bf16[128,1024]{1,0:T(8,128)(2,1)S(1)}, bf16[128,1024]{1,0:T(8,128)(2,1)S(1)}, u32[]{:S(2)}, u32[]{:S(2)}) collective-permute-start(bf16[128,1024]{1,0:T(8,128)(2,1)S(1)} %copy-done.7), channel_id=1, source_target_pairs={{0,3},{1,2},{2,1},{3,0},{4,7},{5,6},{6,5},{7,4},{8,9},{9,8},{10,11... | collective-permute-start | bytes 786440 | tf_op jit(solution)/shard_map/ppermute | solution.py:258
  84.4 23.3 %copy-start.6 = (bf16[2,128,1024]{2,1,0:T(8,128)(2,1)S(1)}, bf16[2,128,1024]{2,1,0:T(8,128)(2,1)}, u32[]{:S(2)}) copy-start(bf16[2,128,1024]{2,1,0:T(8,128)(2,1)} %get-tuple-element.17) | copy-start | bytes 1572868
  85.7 23.1 %copy-start.4 = (bf16[2,128,1024]{2,1,0:T(8,128)(2,1)S(1)}, bf16[2,128,1024]{2,1,0:T(8,128)(2,1)}, u32[]{:S(2)}) copy-start(bf16[2,128,1024]{2,1,0:T(8,128)(2,1)} %get-tuple-element.23) | copy-start | bytes 1572868
  85.7 23.1 %collective-permute-start.7 = (bf16[2,128,1024]{2,1,0:T(8,128)(2,1)S(1)}, bf16[2,128,1024]{2,1,0:T(8,128)(2,1)S(1)}, u32[]{:S(2)}, u32[]{:S(2)}) collective-permute-start(bf16[2,128,1024]{2,1,0:T(8,128)(2,1)S(1)} %add_convert_fusion.1), channel_id=1, source_target_pairs={{0,4},{1,5},{2,6},{3,7},{4,0},{5,1},{6,2},{7,3},{8,12},{9,13},{10,... | collective-permute-start | bytes 1572872 | tf_op jit(solution)/shard_map/ppermute | solution.py:258
  100.7 10.8 %copy-start.5 = (bf16[2,128,1024]{2,1,0:T(8,128)(2,1)S(1)}, bf16[2,128,1024]{2,1,0:T(8,128)(2,1)}, u32[]{:S(2)}) copy-start(bf16[2,128,1024]{2,1,0:T(8,128)(2,1)} %get-tuple-element.26) | copy-start | bytes 1572868
  100.7 10.8 %collective-permute-start.10 = (bf16[2,128,1024]{2,1,0:T(8,128)(2,1)S(1)}, bf16[2,128,1024]{2,1,0:T(8,128)(2,1)S(1)}, u32[]{:S(2)}, u32[]{:S(2)}) collective-permute-start(bf16[2,128,1024]{2,1,0:T(8,128)(2,1)S(1)} %add_convert_fusion), channel_id=1, source_target_pairs={{0,4},{1,5},{2,6},{3,7},{4,0},{5,1},{6,2},{7,3},{8,12},{9,13},{10,... | collective-permute-start | bytes 1572872 | tf_op jit(solution)/shard_map/ppermute | solution.py:258
  102.3 14.6 %collective-permute-start.5 = (bf16[128,1024]{1,0:T(8,128)(2,1)S(1)}, bf16[128,1024]{1,0:T(8,128)(2,1)S(1)}, u32[]{:S(2)}, u32[]{:S(2)}) collective-permute-start(bf16[128,1024]{1,0:T(8,128)(2,1)S(1)} %fusion.5), channel_id=1, source_target_pairs={{0,3},{1,2},{2,1},{3,0},{4,7},{5,6},{6,5},{7,4},{8,9},{9,8},{10,11... | collective-permute-start | bytes 786440 | tf_op jit(solution)/shard_map/ppermute | solution.py:258
  108.9 8.1 %collective-permute-start.8 = (bf16[128,1024]{1,0:T(8,128)(2,1)S(1)}, bf16[128,1024]{1,0:T(8,128)(2,1)S(1)}, u32[]{:S(2)}, u32[]{:S(2)}) collective-permute-start(bf16[128,1024]{1,0:T(8,128)(2,1)S(1)} %fusion.6), channel_id=1, source_target_pairs={{0,3},{1,2},{2,1},{3,0},{4,7},{5,6},{6,5},{7,4},{8,9},{9,8},{10,11... | collective-permute-start | bytes 786440 | tf_op jit(solution)/shard_map/ppermute | solution.py:258
  111.6 9.7 %collective-permute-start.11 = (bf16[128,1024]{1,0:T(8,128)(2,1)S(1)}, bf16[128,1024]{1,0:T(8,128)(2,1)S(1)}, u32[]{:S(2)}, u32[]{:S(2)}) collective-permute-start(bf16[128,1024]{1,0:T(8,128)(2,1)S(1)} %fusion.7), channel_id=1, source_target_pairs={{0,3},{1,2},{2,1},{3,0},{4,7},{5,6},{6,5},{7,4},{8,9},{9,8},{10,11... | collective-permute-start | bytes 786440 | tf_op jit(solution)/shard_map/ppermute | solution.py:258
where the time goes:
time: 122 us
  Pallas kernels  65.5 us (54%)
  starting transfers between devices  26.6 us (22%)
  waiting for transfers between devices  18 us (15%)
  other arithmetic  10.8 us (9%)
    pallas_call x4, Pallas kernels, partial_sums(): pl.pallas_call(functools.partial(kernel, chunk), grid=(1,), in_specs=[sme...  65.5 us
    ppermute x12, starting transfers between devices, swap(): return lax.ppermute(x, ('dp', 'tp'), pairs)  26.6 us
    ppermute x12, waiting for transfers between devices, swap(): return lax.ppermute(x, ('dp', 'tp'), pairs)  18 us
    convert_element_type x4, other arithmetic, along_x(): return (mine[c][1].astype(f32) + got[c][2:].astype(f32)).astype(bf16)  4.51 us
  transfers between devices with their start and end apart: 12, of which 3 were waited for; matrix products, arithmetic and copies ran while one was open for 7% of the time, Pallas kernels for 40%

commit v1 on v0

v1 whole, which is shorter than its diff:
```python
import functools
import math

import jax
import jax.numpy as jnp
from jax import lax
from jax.experimental import pallas as pl
from jax.experimental.pallas import tpu as pltpu
from jax.sharding import PartitionSpec as P

HEAD_DIM = 128
PAGE = 128
HEADS = 8
HIDDEN = 32
CHUNK = 128
KEYS = 256
GROUP = 32
WIDE = HEADS * CHUNK
COLUMNS = 1024
TILES = 2048 // KEYS
THRESHOLD = 32
NEG = -1e30
SCALE = HEAD_DIM**-0.5
LOG2E = math.log2(math.e)
TO_EXP2 = SCALE * LOG2E
SUMS = 16
MIB = 1 << 20
LIMIT = 50


def column_blocks():
    me = lax.axis_index("tp")
    core = lax.rem(lax.axis_index("dp"), 2)
    hi, z = me // 4, lax.rem(me, 4)
    flip, mirror = z + 1 - 2 * lax.rem(z, 2), 3 - z
    first = jnp.where(core == 0, flip, mirror)
    second = jnp.where(core == 0, mirror, flip)
    both = 3 - first
    both = jnp.where(core == 0, 3 - flip, mirror + 1 - 2 * lax.rem(mirror, 2))
    own, other = hi * 4, (1 - hi) * 4
    return [
        own + first, own + both, other + first, other + both,
        other + z, other + second, own + z, own + second,
    ]


def attention(
    chunk, params, slope_ref, shift_ref, mix_ref, q_ref, kv_ref, qt, acc, peak,
    scores, probs, scale, xs, lines, bits, kinks, att,
):
    start_ref, table_ref, slopes, shifts, mixes = params
    row0 = (start_ref[0] + chunk) * PAGE
    for h in range(HEADS):
        columns = slice(h * 128, (h + 1) * 128)
        scaled = q_ref[:, columns].astype(jnp.float32).T * TO_EXP2
        upper = scaled.astype(jnp.bfloat16)
        qt[:128, columns] = upper
        qt[128:, columns] = (scaled - upper.astype(jnp.float32)).astype(jnp.bfloat16)
    acc[...] = jnp.zeros_like(acc)
    peak[...] = jnp.full_like(peak, NEG)
    probs[1][...] = jnp.zeros_like(probs[1])
    scale[1][...] = jnp.zeros_like(scale[1])
    rows = row0 + lax.broadcasted_iota(jnp.int32, (1, CHUNK), 1)
    rec = 1.0 / jnp.log(1.0 + jnp.maximum(rows, THRESHOLD).astype(jnp.float32))
    ahead = lax.broadcasted_iota(jnp.int32, (KEYS, CHUNK), 1) - lax.broadcasted_iota(
        jnp.int32, (KEYS, CHUNK), 0
    )
    pages = KEYS // PAGE
    tiles = (start_ref[0] + chunk + pages) // pages

    def slots(b):
        return [table_ref[0, jnp.minimum(b * pages + n, 15)] for n in range(pages)]

    gaps = row0 - KEYS * lax.broadcasted_iota(jnp.int32, (TILES, HIDDEN), 0)
    least_log = jnp.log(1.0 + jnp.maximum(gaps - (KEYS - 1), 0).astype(jnp.float32))
    most_log = jnp.log(1.0 + jnp.maximum(gaps + (CHUNK - 1), 0).astype(jnp.float32))
    low = least_log * (jnp.min(rec, axis=1, keepdims=True) * (1 - 1e-5))
    high = most_log * (jnp.max(rec, axis=1, keepdims=True) * (1 + 1e-5))
    slope, shift, mix = slope_ref[...], shift_ref[...], mix_ref[...] * LOG2E
    at_low, at_high = slope * low + shift, slope * high + shift
    least, most = jnp.minimum(at_low, at_high), jnp.maximum(at_low, at_high)
    unit = lax.broadcasted_iota(jnp.int32, (TILES, HIDDEN), 1)
    weight = jnp.left_shift(1, unit & 15).astype(jnp.float32)
    weight = jnp.where((least < 0) & (most > 0), weight, 0.0)
    weights = jnp.where(unit < 16, weight, 0.0), jnp.where(unit < 16, 0.0, weight)
    shift_on, slope_on = jnp.where(least >= 0, shift, 0.0), jnp.where(least >= 0, slope, 0.0)
    for b in range(TILES):
        for n, on in enumerate((shift_on, slope_on)):
            line = jnp.sum(mix * on[b : b + 1], axis=1, keepdims=True)
            lines[b, n] = jnp.broadcast_to(line, (HEADS, CHUNK))
            bits[b, n] = jnp.sum(weights[n][b : b + 1]).astype(jnp.int32)

    def score(b, slot):
        k = jnp.concatenate([kv_ref[s, :, :128] for s in slots(b)], axis=0)
        k = jnp.concatenate([k, k], axis=1)
        for g in range(HEADS // 2):
            columns = slice(g * 256, (g + 1) * 256)
            scores[slot][:, columns] = jnp.dot(k, qt[:, columns], preferred_element_type=jnp.float32)
        gap = row0 - b * KEYS
        xs[slot][...] = jnp.log(1.0 + jnp.maximum(ahead + gap, 0).astype(jnp.float32)) * rec

    def mend(b, slot):
        gap = row0 - b * KEYS
        halves = bits[jnp.minimum(b, TILES - 1), 0], bits[jnp.minimum(b, TILES - 1), 1]

        @pl.when((halves[0] + halves[1] > 0) | (gap < KEYS - 1))
        def _():
            bent = jnp.int32(0)
            for f in range(HIDDEN):
                kinks[bent] = f
                bent = bent + (lax.shift_right_logical(halves[f // 16], f % 16) & 1)
            kinks[bent] = 0

            def group(n, carry):
                at = pl.ds(pl.multiple_of(n * GROUP, GROUP), GROUP)
                x = xs[slot][at, :]

                def unit(e, terms):
                    f, g = kinks[2 * e], kinks[2 * e + 1]
                    second = jnp.where(2 * e + 1 < bent, LOG2E, 0.0)
                    one = jnp.maximum((slopes[f] * LOG2E) * x + shifts[f] * LOG2E, 0.0)
                    two = jnp.maximum((slopes[g] * second) * x + shifts[g] * second, 0.0)
                    return tuple(
                        t + (mixes[h, f] * one + mixes[h, g] * two)
                        for h, t in enumerate(terms)
                    )

                terms = tuple(scores[slot][at, h * 128 : (h + 1) * 128] for h in range(HEADS))
                unseen = gap - n * GROUP + CHUNK - 1 < 0
                terms = lax.fori_loop(0, jnp.where(unseen, 0, (bent + 1) // 2), unit, terms)
                seen = ahead[:GROUP] + (gap - n * GROUP) >= 0
                for h in range(HEADS):
                    scores[slot][at, h * 128 : (h + 1) * 128] = jnp.where(seen, terms[h], NEG)
                return carry

            lax.fori_loop(0, KEYS // GROUP, group, 0)

    def weigh(b, slot):
        b = jnp.minimum(b, TILES - 1)
        for h in range(HEADS):
            columns = slice(h * 128, (h + 1) * 128)
            flat = lines[b, 0, h : h + 1]
            t = scores[slot][:, columns] + lines[b, 1, h : h + 1] * xs[slot][...]
            before = peak[h : h + 1]
            after = jnp.maximum(before, jnp.max(t, axis=0, keepdims=True) + flat)
            factor = jnp.exp2(before - after)
            p = jnp.exp2(t - (after - flat))
            peak[h : h + 1] = after
            scale[slot][:, columns] = factor
            probs[slot][:, columns] = p.astype(jnp.bfloat16)

    def gather(b, slot):
        vt = jnp.concatenate([kv_ref[s, :, 128:].T for s in slots(b)], axis=1)
        vt = jnp.concatenate([vt, jnp.ones((SUMS, KEYS), jnp.bfloat16)], axis=0)
        for g in range(HEADS // 2):
            columns = slice(g * 256, (g + 1) * 256)
            update = jnp.dot(vt, probs[slot][:, columns], preferred_element_type=jnp.float32)
            acc[:, columns] = acc[:, columns] * scale[slot][:, columns] + update

    def step(b, slot):
        mend(b, slot)
        score(b + 1, 1 - slot)
        gather(jnp.maximum(b - 1, 0), 1 - slot)
        weigh(b, slot)

    def tile(b, carry):
        for slot in range(2):
            pl.when(b % 2 == slot)(functools.partial(step, b, slot))
        return carry

    score(0, 0)
    lax.fori_loop(0, tiles, tile, 0)
    for slot in range(2):
        pl.when(tiles % 2 != slot)(functools.partial(gather, tiles - 1, slot))
    for h in range(HEADS):
        columns = slice(h * 128, (h + 1) * 128)
        total = acc[128:129, columns]
        att[:, columns] = (acc[:128, columns] / total).T.astype(jnp.bfloat16)


def kernel(chunk, attends, rows, keeps, waits, *refs):
    refs = list(refs)
    take = lambda n: [refs.pop(0) for _ in range(n)]
    inputs = take(10) if attends else []
    (w_ref,) = take(1)
    given = take(1) if rows > CHUNK or not attends else []
    take(waits)
    sends = take(1) if attends else []
    kept = [take(2) for _ in range(rows // CHUNK)] if keeps else []
    handed = [] if keeps else take(1)
    att, wbuf, stage, fetched, stored = take(5)
    blocks = column_blocks()
    first, last = (0 if attends else 4), (8 if keeps else 4)

    def fetch(n):
        columns = pl.ds(pl.multiple_of(blocks[n] * COLUMNS, COLUMNS), COLUMNS)
        return pltpu.make_async_copy(w_ref.at[:, columns], wbuf.at[n - first], fetched.at[n - first])

    for n in range(first, last):
        fetch(n).start()
    if given:
        att[:CHUNK] = given[0][...]
    own = slice(rows - CHUNK, rows)
    if attends:
        qt, acc, peak, s0, s1, p0, p1, f0, f1, x0, x1, lines, bits, kinks = take(14)
        attention(
            chunk, inputs[:5], *inputs[5:], qt, acc, peak, (s0, s1), (p0, p1), (f0, f1),
            (x0, x1), lines, bits, kinks, att.at[own],
        )
    copies = []

    def store(start, count, ref):
        n = len(copies)
        copies.append(pltpu.make_async_copy(stage.at[start : start + count], ref, stored.at[n]))
        copies[-1].start()

    if attends:
        for n in range(4):
            fetch(n).wait()

        def send(n, carry):
            product = jnp.dot(att[own], wbuf[n], preferred_element_type=jnp.float32)
            stage[n] = product.astype(jnp.bfloat16)
            return carry

        lax.fori_loop(0, 4, send, 0)
        store(0, 4, sends[0])
    if not keeps:
        copies.append(pltpu.make_async_copy(att, handed[0], stored.at[1]))
        copies[-1].start()
    for half in range(2 if keeps else 0):
        for n in range(2):
            fetch(4 + 2 * half + n).wait()

        def keep(n, carry, half=half):
            product = jnp.dot(
                att[...], wbuf[4 - first + 2 * half + n], preferred_element_type=jnp.float32
            ).astype(jnp.bfloat16)
            for r in range(rows // CHUNK):
                stage[4 + 2 * half + n + 4 * r] = product[r * CHUNK : (r + 1) * CHUNK]
            return carry

        lax.fori_loop(0, 2, keep, 0)
        for r in range(rows // CHUNK):
            store(4 + 2 * half + 4 * r, 2, kept[r][half])
    for copy in copies:
        copy.wait()


def partial_sums(chunk, attends, keeps, w, inputs=(), given=(), after=()):
    smem = pl.BlockSpec(memory_space=pltpu.SMEM)
    anywhere = pl.BlockSpec(memory_space=pl.ANY)
    whole = pl.BlockSpec(memory_space=pltpu.VMEM)
    rows = CHUNK * (int(attends) + len(given))
    blocks = lambda n: jax.ShapeDtypeStruct((n, CHUNK, COLUMNS), jnp.bfloat16)
    wanted = 4 * (int(attends) + int(keeps))
    in_specs, out_shape, scratch = [], [], []
    if attends:
        in_specs += [smem] * 5 + [whole] * 3
        in_specs += [pl.BlockSpec((CHUNK, HEADS * 128), lambda i: (chunk, 0)), whole]
        out_shape += [blocks(4)]
        scratch += [
            pltpu.VMEM((256, WIDE), jnp.bfloat16),
            pltpu.VMEM((128 + SUMS, WIDE), jnp.float32),
            pltpu.VMEM((HEADS, CHUNK), jnp.float32),
        ]
        scratch += [pltpu.VMEM((KEYS, WIDE), jnp.float32)] * 2
        scratch += [pltpu.VMEM((KEYS, WIDE), jnp.bfloat16)] * 2
        scratch += [pltpu.VMEM((1, WIDE), jnp.float32)] * 2
        scratch += [pltpu.VMEM((KEYS, CHUNK), jnp.float32)] * 2
        scratch += [
            pltpu.VMEM((TILES, 2, HEADS, CHUNK), jnp.float32),
            pltpu.SMEM((TILES, 2), jnp.int32),
            pltpu.SMEM((HIDDEN + 1,), jnp.int32),
        ]
    in_specs += [anywhere] + [whole] * len(given) + [anywhere] * len(after)
    if keeps:
        out_shape += [blocks(2)] * (2 * rows // CHUNK)
    else:
        out_shape += [jax.ShapeDtypeStruct((CHUNK, HEADS * 128), jnp.bfloat16)]
    return pl.pallas_call(
        functools.partial(kernel, chunk, attends, rows, keeps, len(after)),
        grid=(1,),
        in_specs=in_specs,
        out_specs=[anywhere] * len(out_shape),
        out_shape=out_shape,
        scratch_shapes=[
            pltpu.VMEM((rows, HEADS * 128), jnp.bfloat16),
            pltpu.VMEM((wanted, HEADS * 128, COLUMNS), jnp.bfloat16),
            pltpu.VMEM((4 + 4 * rows // CHUNK, CHUNK, COLUMNS), jnp.bfloat16),
            pltpu.SemaphoreType.DMA((wanted,)),
            pltpu.SemaphoreType.DMA((5,)),
        ]
        + scratch,
        compiler_params=pltpu.CompilerParams(vmem_limit_bytes=(60 if chunk == 0 else LIMIT) * MIB),
        cost_estimate=pl.CostEstimate(
            flops=10 * 10**9 if attends else 4 * 10**9,
            bytes_accessed=wanted * 2 * MIB + 4 * MIB,
            transcendentals=CHUNK * 2048 * 8 if attends else 0,
        ),
        name=f"chunk{chunk}" if attends else f"rest{chunk}",
    )(*inputs, w, *given, *after)


def add(terms, after):
    arrays = [x for x, _, _ in terms]
    if after:
        arrays[0] = lax.optimization_barrier((arrays[0], *after))[0]
    total = 0.0
    for x, (_, first, last) in zip(arrays, terms):
        total = total + x[first:last].astype(jnp.float32)
    return total.astype(jnp.bfloat16)


def swap(x, step):
    pairs = []
    for dp in range(16):
        for hi in range(2):
            for z in range(4):
                if step == 1:
                    to = (1 - hi) * 4 + z
                else:
                    to = hi * 4 + ((z ^ 1) if (dp + step // 2) % 2 == 0 else 3 - z)
                pairs.append((dp * 8 + hi * 4 + z, dp * 8 + to))
    return lax.ppermute(x, ("dp", "tp"), pairs)


def shards(queries, kv_pool, span_start, page_table, fire_slope, fire_shift, fire_mix, out_weight):
    mix = fire_mix.T
    inputs = (
        span_start, page_table, fire_slope, fire_shift, mix,
        fire_slope[None], fire_shift[None], mix, queries, kv_pool,
    )
    chunks = queries.shape[0] // CHUNK
    sent, cross, keep, got, got_x, got_z, crossed, last = ([None] * chunks for _ in range(8))

    def along_x(c, after=()):
        crossed[c] = add([(cross[c], 0, 2), (got[c], 2, 4)], after)
        got_x[c] = swap(crossed[c], 1)

    def along_z(c, after=()):
        last[c] = add([(keep[c], 1, 2), (got[c], 1, 2), (got_x[c], 1, 2)], after)
        got_z[c] = swap(last[c], 2)

    def run(c, attends, keeps, given=(), after=()):
        outs = partial_sums(c, attends, keeps, out_weight, inputs if attends else (), given, after)
        if attends:
            sent[c] = outs[0]
            got[c] = swap(sent[c], 0)
            outs = outs[1:]
        if keeps:
            for r, at in enumerate(range(c - (len(outs) // 2 - 1), c + 1)):
                cross[at], keep[at] = outs[2 * r : 2 * r + 2]
        return outs

    (held,) = run(0, True, False)
    run(1, True, True, [held], [sent[0]])
    along_x(0, [sent[1]])
    run(2, True, True, (), [crossed[0]])
    along_x(1, [sent[2]])
    along_z(0, [crossed[1]])
    (held,) = run(3, True, False, (), [last[0]])
    along_x(2, [sent[3]])
    along_z(1, [crossed[2]])
    run(3, False, True, [held], [last[1]])
    along_x(3)
    along_z(2, [crossed[3]])
    along_z(3, [last[2]])
    outs = [
        (
            keep[c][0].astype(jnp.float32)
            + got[c][0].astype(jnp.float32)
            + got_x[c][0].astype(jnp.float32)
            + got_z[c][0].astype(jnp.float32)
        ).astype(jnp.bfloat16)
        for c in range(chunks)
    ]
    return jnp.concatenate(outs, axis=0)


def solution(mesh):
    in_specs = (
        P("dp", "tp"),
        P("dp", None, "tp"),
        P("dp"),
        P("dp", None),
        P(),
        P(),
        P(None, "tp"),
        P("tp", None),
    )
    out_specs = P("dp", "tp")
    return jax.shard_map(shards, mesh=mesh, in_specs=in_specs, out_specs=out_specs, check_vma=False)
```

time: 122 us -> 106 us (0.87)
  the two profiles are of different devices: /device:TPU:18 before, /device:TPU:9 now
where the time goes in v1:
time: 106 us; the launch traced here: 108 us
  Pallas kernels  62.6 us (59%)
  waiting for transfers between devices  25.2 us (24%)
  starting transfers between devices  15.4 us (15%)
  other arithmetic  2.96 us (3%)
    pallas_call x5, Pallas kernels, partial_sums(): pl.pallas_call(functools.partial(kernel, chunk, attends, rows, keeps, len...  62.6 us
    ppermute x12, waiting for transfers between devices, swap(): return lax.ppermute(x, ('dp', 'tp'), pairs)  25.2 us
    ppermute x12, starting transfers between devices, swap(): return lax.ppermute(x, ('dp', 'tp'), pairs)  15.4 us
  transfers between devices with their start and end apart: 12, of which 5 were waited for; matrix products, arithmetic and copies ran while one was open for 2% of the time, Pallas kernels for 45%

profile of v1, /device:TPU:9, one launch (start us, length us, event | category | flops | bytes accessed | tf_op | source)
XLA Modules:
  0.0 108.0 jit_solution(8624469591718458349)
XLA Ops:
  0.7 14.0 %chunk0.1 = (bf16[4,128,1024]{2,1,0:T(8,128)(2,1)}, bf16[128,1024]{1,0:T(8,128)(2,1)}) custom-call(s32[1]{0:T(128)S(6)} %copy.9.refs_0_, s32[1,16]{1,0:T(1,128)} %refs_1_.7, f32[32]{0:T(128)} %refs_2_.7, f32[32]{0:T(128)} %refs_3_.7, f32[8,32]{1,0:T(8,128)} %bitcast.11, f32[1,32]{1,0:T(1,128)} %bitcast.19, f32[1,32]{1,0:T(1,128)} %bitcast.23, ...), custom_call_target="tpu_custom_call" | custom-call | flops 10000000000 | bytes 12582912 | tf_op jit(solution)/shard_map/chunk0/pallas_call | solution.py:281
  14.7 3.8 %collective-permute-start = (bf16[4,128,1024]{2,1,0:T(8,128)(2,1)}, bf16[4,128,1024]{2,1,0:T(8,128)(2,1)S(1)}, u32[]{:S(2)}, u32[]{:S(2)}) collective-permute-start(bf16[4,128,1024]{2,1,0:T(8,128)(2,1)} %get-tuple-element.27.refs_12_), channel_id=1, source_target_pairs={{0,1},{1,0},{2,3},{3,2},{4,5},{5,4},{6,7},{7,6},{8,11},{9,10},{10,... | collective-permute-start | bytes 3145736 | tf_op jit(solution)/shard_map/ppermute | solution.py:325
  18.5 0.9 copy-done.6
  19.5 15.6 %chunk1.1 = (bf16[4,128,1024]{2,1,0:T(8,128)(2,1)S(1)}, bf16[2,128,1024]{2,1,0:T(8,128)(2,1)S(1)}, bf16[2,128,1024]{2,1,0:T(8,128)(2,1)S(1)}, bf16[2,128,1024]{2,1,0:T(8,128)(2,1)S(1)}, bf16[2,128,1024]{2,1,0:T(8,128)(2,1)S(1)}) custom-call(s32[1]{0:T(128)S(6)} %copy.9.refs_0_, s32[1,16]{1,0:T(1,128)S(1)} %copy-done.3, f32[32]{0:T(128)S(1)} %copy-done.4, ...), custom_call_target="tpu_custom_call" | custom-call | flops 10000000000 | bytes 20971520 | tf_op jit(solution)/shard_map/chunk1/pallas_call | solution.py:281
  35.1 0.1 collective-permute-start.2
  35.2 0.2 add_convert_fusion.3.refs_11_
  35.4 2.8 %collective-permute-start.1 = (bf16[2,128,1024]{2,1,0:T(8,128)(2,1)S(1)}, bf16[2,128,1024]{2,1,0:T(8,128)(2,1)S(1)}, u32[]{:S(2)}, u32[]{:S(2)}) collective-permute-start(bf16[2,128,1024]{2,1,0:T(8,128)(2,1)S(1)} %add_convert_fusion.3.refs_11_), channel_id=1, source_target_pairs={{0,4},{1,5},{2,6},{3,7},{4,0},{5,1},{6,2},{7,3},{8,12},{9,13},{10,... | collective-permute-start | bytes 1572872 | tf_op jit(solution)/shard_map/ppermute | solution.py:325
  38.2 16.1 %chunk2.1 = (bf16[4,128,1024]{2,1,0:T(8,128)(2,1)S(1)}, bf16[2,128,1024]{2,1,0:T(8,128)(2,1)S(1)}, bf16[2,128,1024]{2,1,0:T(8,128)(2,1)S(1)}) custom-call(s32[1]{0:T(128)S(6)} %copy.9.refs_0_, s32[1,16]{1,0:T(1,128)S(1)} %copy-done.3, f32[32]{0:T(128)S(1)} %copy-done.4, f32[32]{0:T(128)S(1)} %copy-done.5, f32[8,32]{1,0:T(8,128)S(1)} %bitcast.15, ...), custom_call_target="tpu_custom_call" | custom-call | flops 10000000000 | bytes 20971520 | tf_op jit(solution)/shard_map/chunk2/pallas_call | solution.py:281
  54.3 2.7 %collective-permute-start.5 = (bf16[4,128,1024]{2,1,0:T(8,128)(2,1)S(1)}, bf16[4,128,1024]{2,1,0:T(8,128)(2,1)S(1)}, u32[]{:S(2)}, u32[]{:S(2)}) collective-permute-start(bf16[4,128,1024]{2,1,0:T(8,128)(2,1)S(1)} %get-tuple-element.33), channel_id=1, source_target_pairs={{0,1},{1,0},{2,3},{3,2},{4,5},{5,4},{6,7},{7,6},{8,11},{9,10},{10,... | collective-permute-start | bytes 3145736 | tf_op jit(solution)/shard_map/ppermute | solution.py:325
  57.0 0.2 add_convert_fusion.2
  57.2 0.5 collective-permute-start.4
  57.7 0.1 add_convert_fusion.11.refs_11_
  57.9 12.4 %chunk3.1 = (bf16[4,128,1024]{2,1,0:T(8,128)(2,1)S(1)}, bf16[128,1024]{1,0:T(8,128)(2,1)S(1)}) custom-call(s32[1]{0:T(128)S(6)} %copy.9.refs_0_, s32[1,16]{1,0:T(1,128)S(1)} %copy-done.3, f32[32]{0:T(128)S(1)} %copy-done.4, f32[32]{0:T(128)S(1)} %copy-done.5, f32[8,32]{1,0:T(8,128)S(1)} %bitcast.17, f32[1,32]{1,0:T(1,128)S(1)} %bitcast.22, ...), custom_call_target="tpu_custom_call" | custom-call | flops 10000000000 | bytes 12582912 | tf_op jit(solution)/shard_map/chunk3/pallas_call | solution.py:281
  70.3 0.4 collective-permute-start.8
  70.6 1.8 %collective-permute-done.5 = bf16[4,128,1024]{2,1,0:T(8,128)(2,1)S(1)} collective-permute-done((bf16[4,128,1024]{2,1,0:T(8,128)(2,1)S(1)}, bf16[4,128,1024]{2,1,0:T(8,128)(2,1)S(1)}, u32[]{:S(2)}, u32[]{:S(2)}) %collective-permute-start.5) | collective-permute-done | bytes 1048608 | tf_op jit(solution)/shard_map/ppermute | solution.py:325
  72.4 0.2 add_convert_fusion.1
  72.6 0.9 collective-permute-start.7
  73.5 0.1 add_convert_fusion.9.refs_2_
  73.6 4.5 %rest3.1 = (bf16[2,128,1024]{2,1,0:T(8,128)(2,1)S(1)}, bf16[2,128,1024]{2,1,0:T(8,128)(2,1)S(1)}) custom-call(bf16[1024,8192]{1,0:T(8,128)(2,1)} %refs_0_.5, bf16[128,1024]{1,0:T(8,128)(2,1)S(1)} %get-tuple-element.42.refs_1_, bf16[1,128,1024]{2,1,0:T(8,128)(2,1)S(1)} %add_convert_fusion.9.refs_2_), custom_call_target="tpu_custom_call" | custom-call | flops 4000000000 | bytes 12582912 | tf_op jit(solution)/shard_map/rest3/pallas_call | solution.py:281
  78.1 13.4 %collective-permute-done.8 = bf16[4,128,1024]{2,1,0:T(8,128)(2,1)S(1)} collective-permute-done((bf16[4,128,1024]{2,1,0:T(8,128)(2,1)S(1)}, bf16[4,128,1024]{2,1,0:T(8,128)(2,1)S(1)}, u32[]{:S(2)}, u32[]{:S(2)}) %collective-permute-start.8) | collective-permute-done | bytes 1048608 | tf_op jit(solution)/shard_map/ppermute | solution.py:325
  91.5 0.2 add_convert_fusion
  91.7 2.5 %collective-permute-start.10 = (bf16[2,128,1024]{2,1,0:T(8,128)(2,1)S(1)}, bf16[2,128,1024]{2,1,0:T(8,128)(2,1)S(1)}, u32[]{:S(2)}, u32[]{:S(2)}) collective-permute-start(bf16[2,128,1024]{2,1,0:T(8,128)(2,1)S(1)} %add_convert_fusion), channel_id=1, source_target_pairs={{0,4},{1,5},{2,6},{3,7},{4,0},{5,1},{6,2},{7,3},{8,12},{9,13},{10,... | collective-permute-start | bytes 1572872 | tf_op jit(solution)/shard_map/ppermute | solution.py:325
  94.2 0.2 fusion
  94.5 0.1 add_convert_fusion.7
  94.6 1.5 %collective-permute-start.9 = (bf16[1,128,1024]{2,1,0:T(8,128)(2,1)S(1)}, bf16[1,128,1024]{2,1,0:T(8,128)(2,1)S(1)}, u32[]{:S(2)}, u32[]{:S(2)}) collective-permute-start(bf16[1,128,1024]{2,1,0:T(8,128)(2,1)S(1)} %add_convert_fusion.7), channel_id=1, source_target_pairs={{0,3},{1,2},{2,1},{3,0},{4,7},{5,6},{6,5},{7,4},{8,9},{9,8},{10,11... | collective-permute-start | bytes 786440 | tf_op jit(solution)/shard_map/ppermute | solution.py:325
  96.2 5.2 %collective-permute-done.10 = bf16[2,128,1024]{2,1,0:T(8,128)(2,1)S(1)} collective-permute-done((bf16[2,128,1024]{2,1,0:T(8,128)(2,1)S(1)}, bf16[2,128,1024]{2,1,0:T(8,128)(2,1)S(1)}, u32[]{:S(2)}, u32[]{:S(2)}) %collective-permute-start.10) | collective-permute-done | bytes 524320 | tf_op jit(solution)/shard_map/ppermute | solution.py:325
  101.6 0.2 fusion.1
  101.8 0.7 collective-permute-done.9
  102.5 0.2 fusion.2
  102.7 4.1 %collective-permute-done.11 = bf16[1,128,1024]{2,1,0:T(8,128)(2,1)S(1)} collective-permute-done((bf16[1,128,1024]{2,1,0:T(8,128)(2,1)S(1)}, bf16[1,128,1024]{2,1,0:T(8,128)(2,1)S(1)}, u32[]{:S(2)}, u32[]{:S(2)}) %collective-permute-start.11) | collective-permute-done | bytes 262176 | tf_op jit(solution)/shard_map/ppermute | solution.py:325
  106.8 0.2 fusion.3
  107.0 1.0 pad_maximum_fusion
  (24 shorter events, 0.3 us)
Async XLA Ops:
  0.7 17.9 %copy-start.2 = (f32[32,8]{0,1:T(8,128)S(1)}, f32[32,8]{0,1:T(8,128)}, u32[]{:S(2)}) copy-start(f32[32,8]{0,1:T(8,128)} %param.14) | copy-start | bytes 3076
  0.7 17.9 %copy-start.3 = (s32[1,16]{1,0:T(1,128)S(1)}, s32[1,16]{1,0:T(1,128)}, u32[]{:S(2)}) copy-start(s32[1,16]{1,0:T(1,128)} %refs_1_.7) | copy-start | bytes 196
  0.7 17.9 %copy-start.4 = (f32[32]{0:T(128)S(1)}, f32[32]{0:T(128)}, u32[]{:S(2)}) copy-start(f32[32]{0:T(128)} %refs_2_.7) | copy-start | bytes 388
  0.7 17.8 %copy-start.5 = (f32[32]{0:T(128)S(1)}, f32[32]{0:T(128)}, u32[]{:S(2)}) copy-start(f32[32]{0:T(128)} %refs_3_.7) | copy-start | bytes 388
  14.7 20.5 %collective-permute-start = (bf16[4,128,1024]{2,1,0:T(8,128)(2,1)}, bf16[4,128,1024]{2,1,0:T(8,128)(2,1)S(1)}, u32[]{:S(2)}, u32[]{:S(2)}) collective-permute-start(bf16[4,128,1024]{2,1,0:T(8,128)(2,1)} %get-tuple-element.27.refs_12_), channel_id=1, source_target_pairs={{0,1},{1,0},{2,3},{3,2},{4,5},{5,4},{6,7},{7,6},{8,11},{9,10},{10,... | collective-permute-start | bytes 3145736 | tf_op jit(solution)/shard_map/ppermute | solution.py:325
  18.5 1.0 copy-start.6
  19.5 18.7 %copy-start = (bf16[512,1024]{1,0:T(8,128)(2,1)S(1)}, bf16[512,1024]{1,0:T(8,128)(2,1)}, u32[]{:S(2)}) copy-start(bf16[512,1024]{1,0:T(8,128)(2,1)} %refs_8_.7) | copy-start | bytes 3145732
  35.1 22.0 %collective-permute-start.2 = (bf16[4,128,1024]{2,1,0:T(8,128)(2,1)S(1)}, bf16[4,128,1024]{2,1,0:T(8,128)(2,1)S(1)}, u32[]{:S(2)}, u32[]{:S(2)}) collective-permute-start(bf16[4,128,1024]{2,1,0:T(8,128)(2,1)S(1)} %get-tuple-element.30), channel_id=1, source_target_pairs={{0,1},{1,0},{2,3},{3,2},{4,5},{5,4},{6,7},{7,6},{8,11},{9,10},{10,... | collective-permute-start | bytes 3145736 | tf_op jit(solution)/shard_map/ppermute | solution.py:325
  35.4 22.4 %collective-permute-start.1 = (bf16[2,128,1024]{2,1,0:T(8,128)(2,1)S(1)}, bf16[2,128,1024]{2,1,0:T(8,128)(2,1)S(1)}, u32[]{:S(2)}, u32[]{:S(2)}) collective-permute-start(bf16[2,128,1024]{2,1,0:T(8,128)(2,1)S(1)} %add_convert_fusion.3.refs_11_), channel_id=1, source_target_pairs={{0,4},{1,5},{2,6},{3,7},{4,0},{5,1},{6,2},{7,3},{8,12},{9,13},{10,... | collective-permute-start | bytes 1572872 | tf_op jit(solution)/shard_map/ppermute | solution.py:325
  54.3 3.6 %copy-start.1 = (bf16[16,128,256]{2,1,0:T(8,128)(2,1)S(1)}, bf16[16,128,256]{2,1,0:T(8,128)(2,1)}, u32[]{:S(2)}) copy-start(bf16[16,128,256]{2,1,0:T(8,128)(2,1)} %refs_9_.7) | copy-start | bytes 3145732
  54.3 18.0 %collective-permute-start.5 = (bf16[4,128,1024]{2,1,0:T(8,128)(2,1)S(1)}, bf16[4,128,1024]{2,1,0:T(8,128)(2,1)S(1)}, u32[]{:S(2)}, u32[]{:S(2)}) collective-permute-start(bf16[4,128,1024]{2,1,0:T(8,128)(2,1)S(1)} %get-tuple-element.33), channel_id=1, source_target_pairs={{0,1},{1,0},{2,3},{3,2},{4,5},{5,4},{6,7},{7,6},{8,11},{9,10},{10,... | collective-permute-start | bytes 3145736 | tf_op jit(solution)/shard_map/ppermute | solution.py:325
  57.2 16.2 %collective-permute-start.4 = (bf16[2,128,1024]{2,1,0:T(8,128)(2,1)S(1)}, bf16[2,128,1024]{2,1,0:T(8,128)(2,1)S(1)}, u32[]{:S(2)}, u32[]{:S(2)}) collective-permute-start(bf16[2,128,1024]{2,1,0:T(8,128)(2,1)S(1)} %add_convert_fusion.2), channel_id=1, source_target_pairs={{0,4},{1,5},{2,6},{3,7},{4,0},{5,1},{6,2},{7,3},{8,12},{9,13},{10,... | collective-permute-start | bytes 1572872 | tf_op jit(solution)/shard_map/ppermute | solution.py:325
  70.3 21.3 %collective-permute-start.8 = (bf16[4,128,1024]{2,1,0:T(8,128)(2,1)S(1)}, bf16[4,128,1024]{2,1,0:T(8,128)(2,1)S(1)}, u32[]{:S(2)}, u32[]{:S(2)}) collective-permute-start(bf16[4,128,1024]{2,1,0:T(8,128)(2,1)S(1)} %get-tuple-element.38), channel_id=1, source_target_pairs={{0,1},{1,0},{2,3},{3,2},{4,5},{5,4},{6,7},{7,6},{8,11},{9,10},{10,... | collective-permute-start | bytes 3145736 | tf_op jit(solution)/shard_map/ppermute | solution.py:325
  70.6 23.6 %collective-permute-start.3 = (bf16[1,128,1024]{2,1,0:T(8,128)(2,1)S(1)}, bf16[1,128,1024]{2,1,0:T(8,128)(2,1)S(1)}, u32[]{:S(2)}, u32[]{:S(2)}) collective-permute-start(bf16[1,128,1024]{2,1,0:T(8,128)(2,1)S(1)} %add_convert_fusion.11.refs_11_), channel_id=1, source_target_pairs={{0,3},{1,2},{2,1},{3,0},{4,7},{5,6},{6,5},{7,4},{8,9},{9,8},{10,11... | collective-permute-start | bytes 786440 | tf_op jit(solution)/shard_map/ppermute | solution.py:325
  72.6 21.9 %collective-permute-start.7 = (bf16[2,128,1024]{2,1,0:T(8,128)(2,1)S(1)}, bf16[2,128,1024]{2,1,0:T(8,128)(2,1)S(1)}, u32[]{:S(2)}, u32[]{:S(2)}) collective-permute-start(bf16[2,128,1024]{2,1,0:T(8,128)(2,1)S(1)} %add_convert_fusion.1), channel_id=1, source_target_pairs={{0,4},{1,5},{2,6},{3,7},{4,0},{5,1},{6,2},{7,3},{8,12},{9,13},{10,... | collective-permute-start | bytes 1572872 | tf_op jit(solution)/shard_map/ppermute | solution.py:325
  91.7 9.6 %collective-permute-start.10 = (bf16[2,128,1024]{2,1,0:T(8,128)(2,1)S(1)}, bf16[2,128,1024]{2,1,0:T(8,128)(2,1)S(1)}, u32[]{:S(2)}, u32[]{:S(2)}) collective-permute-start(bf16[2,128,1024]{2,1,0:T(8,128)(2,1)S(1)} %add_convert_fusion), channel_id=1, source_target_pairs={{0,4},{1,5},{2,6},{3,7},{4,0},{5,1},{6,2},{7,3},{8,12},{9,13},{10,... | collective-permute-start | bytes 1572872 | tf_op jit(solution)/shard_map/ppermute | solution.py:325
  94.4 7.2 %collective-permute-start.6 = (bf16[1,128,1024]{2,1,0:T(8,128)(2,1)S(1)}, bf16[1,128,1024]{2,1,0:T(8,128)(2,1)S(1)}, u32[]{:S(2)}, u32[]{:S(2)}) collective-permute-start(bf16[1,128,1024]{2,1,0:T(8,128)(2,1)S(1)} %add_convert_fusion.9.refs_2_), channel_id=1, source_target_pairs={{0,3},{1,2},{2,1},{3,0},{4,7},{5,6},{6,5},{7,4},{8,9},{9,8},{10,11... | collective-permute-start | bytes 786440 | tf_op jit(solution)/shard_map/ppermute | solution.py:325
  94.6 7.9 %collective-permute-start.9 = (bf16[1,128,1024]{2,1,0:T(8,128)(2,1)S(1)}, bf16[1,128,1024]{2,1,0:T(8,128)(2,1)S(1)}, u32[]{:S(2)}, u32[]{:S(2)}) collective-permute-start(bf16[1,128,1024]{2,1,0:T(8,128)(2,1)S(1)} %add_convert_fusion.7), channel_id=1, source_target_pairs={{0,3},{1,2},{2,1},{3,0},{4,7},{5,6},{6,5},{7,4},{8,9},{9,8},{10,11... | collective-permute-start | bytes 786440 | tf_op jit(solution)/shard_map/ppermute | solution.py:325
  101.5 5.3 %collective-permute-start.11 = (bf16[1,128,1024]{2,1,0:T(8,128)(2,1)S(1)}, bf16[1,128,1024]{2,1,0:T(8,128)(2,1)S(1)}, u32[]{:S(2)}, u32[]{:S(2)}) collective-permute-start(bf16[1,128,1024]{2,1,0:T(8,128)(2,1)S(1)} %add_convert_fusion.5), channel_id=1, source_target_pairs={{0,3},{1,2},{2,1},{3,0},{4,7},{5,6},{6,5},{7,4},{8,9},{9,8},{10,11... | collective-permute-start | bytes 786440 | tf_op jit(solution)/shard_map/ppermute | solution.py:325

commit v2 on v1

--- a/solution.py
+++ b/solution.py
@@ -183,7 +183,7 @@
     take = lambda n: [refs.pop(0) for _ in range(n)]
     inputs = take(10) if attends else []
     (w_ref,) = take(1)
-    given = take(1) if rows > CHUNK or not attends else []
+    given = take(rows // CHUNK - int(attends))
     take(waits)
     sends = take(1) if attends else []
     kept = [take(2) for _ in range(rows // CHUNK)] if keeps else []
@@ -198,8 +198,8 @@
 
     for n in range(first, last):
         fetch(n).start()
-    if given:
-        att[:CHUNK] = given[0][...]
+    for r, ref in enumerate(given):
+        att[r * CHUNK : (r + 1) * CHUNK] = ref[...]
     own = slice(rows - CHUNK, rows)
     if attends:
         qt, acc, peak, s0, s1, p0, p1, f0, f1, x0, x1, lines, bits, kinks = take(14)
@@ -356,14 +356,14 @@
     (held,) = run(0, True, False)
     run(1, True, True, [held], [sent[0]])
     along_x(0, [sent[1]])
-    run(2, True, True, (), [crossed[0]])
+    (held,) = run(2, True, False, (), [crossed[0]])
     along_x(1, [sent[2]])
     along_z(0, [crossed[1]])
-    (held,) = run(3, True, False, (), [last[0]])
-    along_x(2, [sent[3]])
+    held = [held, *run(3, True, False, (), [last[0]])]
+    run(3, False, True, held, [sent[3]])
+    along_x(2)
     along_z(1, [crossed[2]])
-    run(3, False, True, [held], [last[1]])
-    along_x(3)
+    along_x(3, [crossed[2]])
     along_z(2, [crossed[3]])
     along_z(3, [last[2]])
     outs = [
@@ -375,7 +375,8 @@
         ).astype(jnp.bfloat16)
         for c in range(chunks)
     ]
-    return jnp.concatenate(outs, axis=0)
+    whole = jnp.concatenate(outs[:-1] + [jnp.zeros_like(outs[-1])], axis=0)
+    return lax.dynamic_update_slice(whole, outs[-1], ((chunks - 1) * CHUNK, 0))
 
 
 def solution(mesh):

time: 106 us -> 104 us (0.981)
  the two profiles are of different devices: /device:TPU:9 before, /device:TPU:26 now
where the time goes in v2:
time: 104 us; the launch traced here: 105 us
  Pallas kernels  58.3 us (56%)
  starting transfers between devices  24.1 us (23%)
  waiting for transfers between devices  17 us (16%)
  other arithmetic  3.8 us (4%)
    pallas_call x5, Pallas kernels, partial_sums(): pl.pallas_call(functools.partial(kernel, chunk, attends, rows, keeps, len...  58.3 us
    ppermute x12, starting transfers between devices, swap(): return lax.ppermute(x, ('dp', 'tp'), pairs)  24.1 us
    ppermute x12, waiting for transfers between devices, swap(): return lax.ppermute(x, ('dp', 'tp'), pairs)  17 us
  transfers between devices with their start and end apart: 12, of which 4 were waited for; matrix products, arithmetic and copies ran while one was open for 3% of the time, Pallas kernels for 42%

profile of v2, /device:TPU:26, one launch (start us, length us, event | category | flops | bytes accessed | tf_op | source)
XLA Modules:
  0.0 104.9 jit_solution(3623075553159793423)
XLA Ops:
  0.7 13.7 %chunk0.1 = (bf16[4,128,1024]{2,1,0:T(8,128)(2,1)}, bf16[128,1024]{1,0:T(8,128)(2,1)}) custom-call(s32[1]{0:T(128)S(6)} %copy.10.refs_0_, s32[1,16]{1,0:T(1,128)} %refs_1_.7, f32[32]{0:T(128)} %refs_2_.7, f32[32]{0:T(128)} %refs_3_.7, f32[8,32]{1,0:T(8,128)} %bitcast.13, f32[1,32]{1,0:T(1,128)} %bitcast.21, f32[1,32]{1,0:T(1,128)} %bitcast.25, ...), custom_call_target="tpu_custom_call" | custom-call | flops 10000000000 | bytes 12582912 | tf_op jit(solution)/shard_map/chunk0/pallas_call | solution.py:281
  14.4 2.0 %collective-permute-start = (bf16[4,128,1024]{2,1,0:T(8,128)(2,1)}, bf16[4,128,1024]{2,1,0:T(8,128)(2,1)S(1)}, u32[]{:S(2)}, u32[]{:S(2)}) collective-permute-start(bf16[4,128,1024]{2,1,0:T(8,128)(2,1)} %get-tuple-element.28.refs_12_), channel_id=1, source_target_pairs={{0,1},{1,0},{2,3},{3,2},{4,5},{5,4},{6,7},{7,6},{8,11},{9,10},{10,... | collective-permute-start | bytes 3145736 | tf_op jit(solution)/shard_map/ppermute | solution.py:325
  16.4 0.9 copy-done.6
  17.4 14.8 %chunk1.1 = (bf16[4,128,1024]{2,1,0:T(8,128)(2,1)S(1)}, bf16[2,128,1024]{2,1,0:T(8,128)(2,1)S(1)}, bf16[2,128,1024]{2,1,0:T(8,128)(2,1)S(1)}, bf16[2,128,1024]{2,1,0:T(8,128)(2,1)S(1)}, bf16[2,128,1024]{2,1,0:T(8,128)(2,1)S(1)}) custom-call(s32[1]{0:T(128)S(6)} %copy.10.refs_0_, s32[1,16]{1,0:T(1,128)S(1)} %copy-done.3, f32[32]{0:T(128)S(1)} %copy-done.4, ...), custom_call_target="tpu_custom_call" | custom-call | flops 10000000000 | bytes 20971520 | tf_op jit(solution)/shard_map/chunk1/pallas_call | solution.py:281
  32.2 0.2 collective-permute-start.2
  32.4 0.2 add_convert_fusion.3.refs_11_
  32.6 2.2 %collective-permute-start.1 = (bf16[2,128,1024]{2,1,0:T(8,128)(2,1)S(1)}, bf16[2,128,1024]{2,1,0:T(8,128)(2,1)S(1)}, u32[]{:S(2)}, u32[]{:S(2)}) collective-permute-start(bf16[2,128,1024]{2,1,0:T(8,128)(2,1)S(1)} %add_convert_fusion.3.refs_11_), channel_id=1, source_target_pairs={{0,4},{1,5},{2,6},{3,7},{4,0},{5,1},{6,2},{7,3},{8,12},{9,13},{10,... | collective-permute-start | bytes 1572872 | tf_op jit(solution)/shard_map/ppermute | solution.py:325
  34.8 12.7 %chunk2.1 = (bf16[4,128,1024]{2,1,0:T(8,128)(2,1)S(1)}, bf16[128,1024]{1,0:T(8,128)(2,1)S(1)}) custom-call(s32[1]{0:T(128)S(6)} %copy.10.refs_0_, s32[1,16]{1,0:T(1,128)S(1)} %copy-done.3, f32[32]{0:T(128)S(1)} %copy-done.4, f32[32]{0:T(128)S(1)} %copy-done.5, f32[8,32]{1,0:T(8,128)S(1)} %bitcast.17, f32[1,32]{1,0:T(1,128)S(1)} %bitcast.23, ...), custom_call_target="tpu_custom_call" | custom-call | flops 10000000000 | bytes 12582912 | tf_op jit(solution)/shard_map/chunk2/pallas_call | solution.py:281
  47.5 2.0 %collective-permute-start.5 = (bf16[4,128,1024]{2,1,0:T(8,128)(2,1)S(1)}, bf16[4,128,1024]{2,1,0:T(8,128)(2,1)S(1)}, u32[]{:S(2)}, u32[]{:S(2)}) collective-permute-start(bf16[4,128,1024]{2,1,0:T(8,128)(2,1)S(1)} %get-tuple-element.34), channel_id=1, source_target_pairs={{0,1},{1,0},{2,3},{3,2},{4,5},{5,4},{6,7},{7,6},{8,11},{9,10},{10,... | collective-permute-start | bytes 3145736 | tf_op jit(solution)/shard_map/ppermute | solution.py:325
  49.5 0.2 add_convert_fusion.2
  49.7 0.1 add_convert_fusion.11.refs_11_
  49.9 11.7 %chunk3.1 = (bf16[4,128,1024]{2,1,0:T(8,128)(2,1)S(1)}, bf16[128,1024]{1,0:T(8,128)(2,1)S(1)}) custom-call(s32[1]{0:T(128)S(6)} %copy.10.refs_0_, s32[1,16]{1,0:T(1,128)S(1)} %copy-done.3, f32[32]{0:T(128)S(1)} %copy-done.4, f32[32]{0:T(128)S(1)} %copy-done.5, f32[8,32]{1,0:T(8,128)S(1)} %bitcast.19, f32[1,32]{1,0:T(1,128)S(1)} %bitcast.24, ...), custom_call_target="tpu_custom_call" | custom-call | flops 10000000000 | bytes 12582912 | tf_op jit(solution)/shard_map/chunk3/pallas_call | solution.py:281
  61.6 0.2 collective-permute-start.8
  61.8 1.5 %collective-permute-start.4 = (bf16[2,128,1024]{2,1,0:T(8,128)(2,1)S(1)}, bf16[2,128,1024]{2,1,0:T(8,128)(2,1)S(1)}, u32[]{:S(2)}, u32[]{:S(2)}) collective-permute-start(bf16[2,128,1024]{2,1,0:T(8,128)(2,1)S(1)} %add_convert_fusion.2), channel_id=1, source_target_pairs={{0,4},{1,5},{2,6},{3,7},{4,0},{5,1},{6,2},{7,3},{8,12},{9,13},{10,... | collective-permute-start | bytes 1572872 | tf_op jit(solution)/shard_map/ppermute | solution.py:325
  63.2 4.0 %collective-permute-start.3 = (bf16[1,128,1024]{2,1,0:T(8,128)(2,1)S(1)}, bf16[1,128,1024]{2,1,0:T(8,128)(2,1)S(1)}, u32[]{:S(2)}, u32[]{:S(2)}) collective-permute-start(bf16[1,128,1024]{2,1,0:T(8,128)(2,1)S(1)} %add_convert_fusion.11.refs_11_), channel_id=1, source_target_pairs={{0,3},{1,2},{2,1},{3,0},{4,7},{5,6},{6,5},{7,4},{8,9},{9,8},{10,11... | collective-permute-start | bytes 786440 | tf_op jit(solution)/shard_map/ppermute | solution.py:325
  67.3 5.3 %rest3.1 = (bf16[2,128,1024]{2,1,0:T(8,128)(2,1)S(1)}, bf16[2,128,1024]{2,1,0:T(8,128)(2,1)S(1)}, bf16[2,128,1024]{2,1,0:T(8,128)(2,1)S(1)}, bf16[2,128,1024]{2,1,0:T(8,128)(2,1)S(1)}) custom-call(bf16[1024,8192]{1,0:T(8,128)(2,1)} %refs_0_.5, bf16[128,1024]{1,0:T(8,128)(2,1)S(1)} %get-tuple-element.38.refs_1_, ...), custom_call_target="tpu_custom_call" | custom-call | flops 4000000000 | bytes 12582912 | tf_op jit(solution)/shard_map/rest3/pallas_call | solution.py:281
  72.6 0.2 add_convert_fusion.1
  72.8 2.2 %collective-permute-start.7 = (bf16[2,128,1024]{2,1,0:T(8,128)(2,1)S(1)}, bf16[2,128,1024]{2,1,0:T(8,128)(2,1)S(1)}, u32[]{:S(2)}, u32[]{:S(2)}) collective-permute-start(bf16[2,128,1024]{2,1,0:T(8,128)(2,1)S(1)} %add_convert_fusion.1), channel_id=1, source_target_pairs={{0,4},{1,5},{2,6},{3,7},{4,0},{5,1},{6,2},{7,3},{8,12},{9,13},{10,... | collective-permute-start | bytes 1572872 | tf_op jit(solution)/shard_map/ppermute | solution.py:325
  75.1 3.2 %collective-permute-done.4 = bf16[2,128,1024]{2,1,0:T(8,128)(2,1)S(1)} collective-permute-done((bf16[2,128,1024]{2,1,0:T(8,128)(2,1)S(1)}, bf16[2,128,1024]{2,1,0:T(8,128)(2,1)S(1)}, u32[]{:S(2)}, u32[]{:S(2)}) %collective-permute-start.4) | collective-permute-done | bytes 524320 | tf_op jit(solution)/shard_map/ppermute | solution.py:325
  78.3 3.0 %collective-permute-start.6 = (bf16[1,128,1024]{2,1,0:T(8,128)(2,1)S(1)}, bf16[1,128,1024]{2,1,0:T(8,128)(2,1)S(1)}, u32[]{:S(2)}, u32[]{:S(2)}) collective-permute-start(bf16[1,128,1024]{2,1,0:T(8,128)(2,1)S(1)} %add_convert_fusion.9), channel_id=1, source_target_pairs={{0,3},{1,2},{2,1},{3,0},{4,7},{5,6},{6,5},{7,4},{8,9},{9,8},{10,11... | collective-permute-start | bytes 786440 | tf_op jit(solution)/shard_map/ppermute | solution.py:325
  81.4 0.2 add_convert_fusion
  81.6 0.7 collective-permute-start.10
  82.3 0.2 fusion
  82.5 7.0 %collective-permute-done.7 = bf16[2,128,1024]{2,1,0:T(8,128)(2,1)S(1)} collective-permute-done((bf16[2,128,1024]{2,1,0:T(8,128)(2,1)S(1)}, bf16[2,128,1024]{2,1,0:T(8,128)(2,1)S(1)}, u32[]{:S(2)}, u32[]{:S(2)}) %collective-permute-start.7) | collective-permute-done | bytes 524320 | tf_op jit(solution)/shard_map/ppermute | solution.py:325
  89.6 3.0 %collective-permute-start.9 = (bf16[1,128,1024]{2,1,0:T(8,128)(2,1)S(1)}, bf16[1,128,1024]{2,1,0:T(8,128)(2,1)S(1)}, u32[]{:S(2)}, u32[]{:S(2)}) collective-permute-start(bf16[1,128,1024]{2,1,0:T(8,128)(2,1)S(1)} %add_convert_fusion.7), channel_id=1, source_target_pairs={{0,3},{1,2},{2,1},{3,0},{4,7},{5,6},{6,5},{7,4},{8,9},{9,8},{10,11... | collective-permute-start | bytes 786440 | tf_op jit(solution)/shard_map/ppermute | solution.py:325
  92.6 0.2 fusion.1
  92.8 3.5 %collective-permute-done.10 = bf16[2,128,1024]{2,1,0:T(8,128)(2,1)S(1)} collective-permute-done((bf16[2,128,1024]{2,1,0:T(8,128)(2,1)S(1)}, bf16[2,128,1024]{2,1,0:T(8,128)(2,1)S(1)}, u32[]{:S(2)}, u32[]{:S(2)}) %collective-permute-start.10) | collective-permute-done | bytes 524320 | tf_op jit(solution)/shard_map/ppermute | solution.py:325
  96.4 3.0 %collective-permute-start.11 = (bf16[1,128,1024]{2,1,0:T(8,128)(2,1)S(1)}, bf16[1,128,1024]{2,1,0:T(8,128)(2,1)S(1)}, u32[]{:S(2)}, u32[]{:S(2)}) collective-permute-start(bf16[1,128,1024]{2,1,0:T(8,128)(2,1)S(1)} %add_convert_fusion.5), channel_id=1, source_target_pairs={{0,3},{1,2},{2,1},{3,0},{4,7},{5,6},{6,5},{7,4},{8,9},{9,8},{10,11... | collective-permute-start | bytes 786440 | tf_op jit(solution)/shard_map/ppermute | solution.py:325
  99.4 0.2 fusion.2
  99.6 1.2 %maximum_maximum_fusion = bf16[512,1024]{1,0:T(8,128)(2,1)} fusion(bf16[128,1024]{1,0:T(8,128)(2,1)S(1)} %fusion.2, bf16[128,1024]{1,0:T(8,128)(2,1)S(1)} %fusion.1, bf16[128,1024]{1,0:T(8,128)(2,1)S(1)} %fusion, bf16[512]{0:T(512)(128)(2,1)S(1)} %pad.3.clone), kind=kLoop, calls=%fused_computation | loop fusion | flops 4194304 | bytes 1836032 | tf_op jit(solution)/shard_map/concatenate | solution.py:378
  100.8 3.3 %collective-permute-done.11 = bf16[1,128,1024]{2,1,0:T(8,128)(2,1)S(1)} collective-permute-done((bf16[1,128,1024]{2,1,0:T(8,128)(2,1)S(1)}, bf16[1,128,1024]{2,1,0:T(8,128)(2,1)S(1)}, u32[]{:S(2)}, u32[]{:S(2)}) %collective-permute-start.11) | collective-permute-done | bytes 262176 | tf_op jit(solution)/shard_map/ppermute | solution.py:325
  104.1 0.9 fusion.4
  (26 shorter events, 0.4 us)
Async XLA Ops:
  0.7 15.8 %copy-start.2 = (f32[32,8]{0,1:T(8,128)S(1)}, f32[32,8]{0,1:T(8,128)}, u32[]{:S(2)}) copy-start(f32[32,8]{0,1:T(8,128)} %param.14) | copy-start | bytes 3076
  0.7 15.7 %copy-start.3 = (s32[1,16]{1,0:T(1,128)S(1)}, s32[1,16]{1,0:T(1,128)}, u32[]{:S(2)}) copy-start(s32[1,16]{1,0:T(1,128)} %refs_1_.7) | copy-start | bytes 196
  0.7 15.7 %copy-start.4 = (f32[32]{0:T(128)S(1)}, f32[32]{0:T(128)}, u32[]{:S(2)}) copy-start(f32[32]{0:T(128)} %refs_2_.7) | copy-start | bytes 388
  0.7 15.7 %copy-start.5 = (f32[32]{0:T(128)S(1)}, f32[32]{0:T(128)}, u32[]{:S(2)}) copy-start(f32[32]{0:T(128)} %refs_3_.7) | copy-start | bytes 388
  14.4 18.0 %collective-permute-start = (bf16[4,128,1024]{2,1,0:T(8,128)(2,1)}, bf16[4,128,1024]{2,1,0:T(8,128)(2,1)S(1)}, u32[]{:S(2)}, u32[]{:S(2)}) collective-permute-start(bf16[4,128,1024]{2,1,0:T(8,128)(2,1)} %get-tuple-element.28.refs_12_), channel_id=1, source_target_pairs={{0,1},{1,0},{2,3},{3,2},{4,5},{5,4},{6,7},{7,6},{8,11},{9,10},{10,... | collective-permute-start | bytes 3145736 | tf_op jit(solution)/shard_map/ppermute | solution.py:325
  16.4 1.0 copy-start.6
  17.4 17.4 %copy-start = (bf16[512,1024]{1,0:T(8,128)(2,1)S(1)}, bf16[512,1024]{1,0:T(8,128)(2,1)}, u32[]{:S(2)}) copy-start(bf16[512,1024]{1,0:T(8,128)(2,1)} %refs_8_.7) | copy-start | bytes 3145732
  17.4 17.4 %copy-start.1 = (bf16[16,128,256]{2,1,0:T(8,128)(2,1)S(1)}, bf16[16,128,256]{2,1,0:T(8,128)(2,1)}, u32[]{:S(2)}) copy-start(bf16[16,128,256]{2,1,0:T(8,128)(2,1)} %refs_9_.7) | copy-start | bytes 3145732
  32.2 17.3 %collective-permute-start.2 = (bf16[4,128,1024]{2,1,0:T(8,128)(2,1)S(1)}, bf16[4,128,1024]{2,1,0:T(8,128)(2,1)S(1)}, u32[]{:S(2)}, u32[]{:S(2)}) collective-permute-start(bf16[4,128,1024]{2,1,0:T(8,128)(2,1)S(1)} %get-tuple-element.31), channel_id=1, source_target_pairs={{0,1},{1,0},{2,3},{3,2},{4,5},{5,4},{6,7},{7,6},{8,11},{9,10},{10,... | collective-permute-start | bytes 3145736 | tf_op jit(solution)/shard_map/ppermute | solution.py:325
  32.6 17.1 %collective-permute-start.1 = (bf16[2,128,1024]{2,1,0:T(8,128)(2,1)S(1)}, bf16[2,128,1024]{2,1,0:T(8,128)(2,1)S(1)}, u32[]{:S(2)}, u32[]{:S(2)}) collective-permute-start(bf16[2,128,1024]{2,1,0:T(8,128)(2,1)S(1)} %add_convert_fusion.3.refs_11_), channel_id=1, source_target_pairs={{0,4},{1,5},{2,6},{3,7},{4,0},{5,1},{6,2},{7,3},{8,12},{9,13},{10,... | collective-permute-start | bytes 1572872 | tf_op jit(solution)/shard_map/ppermute | solution.py:325
  47.5 25.1 %collective-permute-start.5 = (bf16[4,128,1024]{2,1,0:T(8,128)(2,1)S(1)}, bf16[4,128,1024]{2,1,0:T(8,128)(2,1)S(1)}, u32[]{:S(2)}, u32[]{:S(2)}) collective-permute-start(bf16[4,128,1024]{2,1,0:T(8,128)(2,1)S(1)} %get-tuple-element.34), channel_id=1, source_target_pairs={{0,1},{1,0},{2,3},{3,2},{4,5},{5,4},{6,7},{7,6},{8,11},{9,10},{10,... | collective-permute-start | bytes 3145736 | tf_op jit(solution)/shard_map/ppermute | solution.py:325
  61.6 19.8 %collective-permute-start.8 = (bf16[4,128,1024]{2,1,0:T(8,128)(2,1)S(1)}, bf16[4,128,1024]{2,1,0:T(8,128)(2,1)S(1)}, u32[]{:S(2)}, u32[]{:S(2)}) collective-permute-start(bf16[4,128,1024]{2,1,0:T(8,128)(2,1)S(1)} %get-tuple-element.40.refs_3_), channel_id=1, source_target_pairs={{0,1},{1,0},{2,3},{3,2},{4,5},{5,4},{6,7},{7,6},{8,11},{9,10},{10,... | collective-permute-start | bytes 3145736 | tf_op jit(solution)/shard_map/ppermute | solution.py:325
  61.8 16.4 %collective-permute-start.4 = (bf16[2,128,1024]{2,1,0:T(8,128)(2,1)S(1)}, bf16[2,128,1024]{2,1,0:T(8,128)(2,1)S(1)}, u32[]{:S(2)}, u32[]{:S(2)}) collective-permute-start(bf16[2,128,1024]{2,1,0:T(8,128)(2,1)S(1)} %add_convert_fusion.2), channel_id=1, source_target_pairs={{0,4},{1,5},{2,6},{3,7},{4,0},{5,1},{6,2},{7,3},{8,12},{9,13},{10,... | collective-permute-start | bytes 1572872 | tf_op jit(solution)/shard_map/ppermute | solution.py:325
  63.2 19.0 %collective-permute-start.3 = (bf16[1,128,1024]{2,1,0:T(8,128)(2,1)S(1)}, bf16[1,128,1024]{2,1,0:T(8,128)(2,1)S(1)}, u32[]{:S(2)}, u32[]{:S(2)}) collective-permute-start(bf16[1,128,1024]{2,1,0:T(8,128)(2,1)S(1)} %add_convert_fusion.11.refs_11_), channel_id=1, source_target_pairs={{0,3},{1,2},{2,1},{3,0},{4,7},{5,6},{6,5},{7,4},{8,9},{9,8},{10,11... | collective-permute-start | bytes 786440 | tf_op jit(solution)/shard_map/ppermute | solution.py:325
  72.8 16.6 %collective-permute-start.7 = (bf16[2,128,1024]{2,1,0:T(8,128)(2,1)S(1)}, bf16[2,128,1024]{2,1,0:T(8,128)(2,1)S(1)}, u32[]{:S(2)}, u32[]{:S(2)}) collective-permute-start(bf16[2,128,1024]{2,1,0:T(8,128)(2,1)S(1)} %add_convert_fusion.1), channel_id=1, source_target_pairs={{0,4},{1,5},{2,6},{3,7},{4,0},{5,1},{6,2},{7,3},{8,12},{9,13},{10,... | collective-permute-start | bytes 1572872 | tf_op jit(solution)/shard_map/ppermute | solution.py:325
  78.3 14.3 %collective-permute-start.6 = (bf16[1,128,1024]{2,1,0:T(8,128)(2,1)S(1)}, bf16[1,128,1024]{2,1,0:T(8,128)(2,1)S(1)}, u32[]{:S(2)}, u32[]{:S(2)}) collective-permute-start(bf16[1,128,1024]{2,1,0:T(8,128)(2,1)S(1)} %add_convert_fusion.9), channel_id=1, source_target_pairs={{0,3},{1,2},{2,1},{3,0},{4,7},{5,6},{6,5},{7,4},{8,9},{9,8},{10,11... | collective-permute-start | bytes 786440 | tf_op jit(solution)/shard_map/ppermute | solution.py:325
  81.6 14.7 %collective-permute-start.10 = (bf16[2,128,1024]{2,1,0:T(8,128)(2,1)S(1)}, bf16[2,128,1024]{2,1,0:T(8,128)(2,1)S(1)}, u32[]{:S(2)}, u32[]{:S(2)}) collective-permute-start(bf16[2,128,1024]{2,1,0:T(8,128)(2,1)S(1)} %add_convert_fusion), channel_id=1, source_target_pairs={{0,4},{1,5},{2,6},{3,7},{4,0},{5,1},{6,2},{7,3},{8,12},{9,13},{10,... | collective-permute-start | bytes 1572872 | tf_op jit(solution)/shard_map/ppermute | solution.py:325
  89.6 9.8 %collective-permute-start.9 = (bf16[1,128,1024]{2,1,0:T(8,128)(2,1)S(1)}, bf16[1,128,1024]{2,1,0:T(8,128)(2,1)S(1)}, u32[]{:S(2)}, u32[]{:S(2)}) collective-permute-start(bf16[1,128,1024]{2,1,0:T(8,128)(2,1)S(1)} %add_convert_fusion.7), channel_id=1, source_target_pairs={{0,3},{1,2},{2,1},{3,0},{4,7},{5,6},{6,5},{7,4},{8,9},{9,8},{10,11... | collective-permute-start | bytes 786440 | tf_op jit(solution)/shard_map/ppermute | solution.py:325
  96.4 7.7 %collective-permute-start.11 = (bf16[1,128,1024]{2,1,0:T(8,128)(2,1)S(1)}, bf16[1,128,1024]{2,1,0:T(8,128)(2,1)S(1)}, u32[]{:S(2)}, u32[]{:S(2)}) collective-permute-start(bf16[1,128,1024]{2,1,0:T(8,128)(2,1)S(1)} %add_convert_fusion.5), channel_id=1, source_target_pairs={{0,3},{1,2},{2,1},{3,0},{4,7},{5,6},{6,5},{7,4},{8,9},{9,8},{10,11... | collective-permute-start | bytes 786440 | tf_op jit(solution)/shard_map/ppermute | solution.py:325

commit v3 on v2

--- a/solution.py
+++ b/solution.py
@@ -186,11 +186,12 @@
     given = take(rows // CHUNK - int(attends))
     take(waits)
     sends = take(1) if attends else []
-    kept = [take(2) for _ in range(rows // CHUNK)] if keeps else []
+    kept = [take(len(keeps)) for _ in range(rows // CHUNK)] if keeps else []
     handed = [] if keeps else take(1)
     att, wbuf, stage, fetched, stored = take(5)
     blocks = column_blocks()
-    first, last = (0 if attends else 4), (8 if keeps else 4)
+    first = 0 if attends else 4 + 2 * keeps[0]
+    last = 6 + 2 * keeps[-1] if keeps else 4
 
     def fetch(n):
         columns = pl.ds(pl.multiple_of(blocks[n] * COLUMNS, COLUMNS), COLUMNS)
@@ -228,7 +229,7 @@
     if not keeps:
         copies.append(pltpu.make_async_copy(att, handed[0], stored.at[1]))
         copies[-1].start()
-    for half in range(2 if keeps else 0):
+    for half in keeps:
         for n in range(2):
             fetch(4 + 2 * half + n).wait()
 
@@ -242,7 +243,7 @@
 
         lax.fori_loop(0, 2, keep, 0)
         for r in range(rows // CHUNK):
-            store(4 + 2 * half + 4 * r, 2, kept[r][half])
+            store(4 + 2 * half + 4 * r, 2, kept[r][half - keeps[0]])
     for copy in copies:
         copy.wait()
 
@@ -253,7 +254,7 @@
     whole = pl.BlockSpec(memory_space=pltpu.VMEM)
     rows = CHUNK * (int(attends) + len(given))
     blocks = lambda n: jax.ShapeDtypeStruct((n, CHUNK, COLUMNS), jnp.bfloat16)
-    wanted = 4 * (int(attends) + int(keeps))
+    wanted = 4 * int(attends) + 2 * len(keeps)
     in_specs, out_shape, scratch = [], [], []
     if attends:
         in_specs += [smem] * 5 + [whole] * 3
@@ -275,7 +276,7 @@
         ]
     in_specs += [anywhere] + [whole] * len(given) + [anywhere] * len(after)
     if keeps:
-        out_shape += [blocks(2)] * (2 * rows // CHUNK)
+        out_shape += [blocks(2)] * (len(keeps) * rows // CHUNK)
     else:
         out_shape += [jax.ShapeDtypeStruct((CHUNK, HEADS * 128), jnp.bfloat16)]
     return pl.pallas_call(
@@ -298,7 +299,7 @@
             bytes_accessed=wanted * 2 * MIB + 4 * MIB,
             transcendentals=CHUNK * 2048 * 8 if attends else 0,
         ),
-        name=f"chunk{chunk}" if attends else f"rest{chunk}",
+        name=f"chunk{chunk}" if attends else f"half{keeps[0]}",
     )(*inputs, w, *given, *after)
 
 
@@ -349,20 +350,22 @@
             got[c] = swap(sent[c], 0)
             outs = outs[1:]
         if keeps:
-            for r, at in enumerate(range(c - (len(outs) // 2 - 1), c + 1)):
-                cross[at], keep[at] = outs[2 * r : 2 * r + 2]
+            count = len(outs) // len(keeps)
+            for n, out in enumerate(outs):
+                (cross, keep)[keeps[n % len(keeps)]][c + 1 - count + n // len(keeps)] = out
         return outs
 
-    (held,) = run(0, True, False)
-    run(1, True, True, [held], [sent[0]])
+    (held,) = run(0, True, ())
+    run(1, True, (0, 1), [held], [sent[0]])
     along_x(0, [sent[1]])
-    (held,) = run(2, True, False, (), [crossed[0]])
-    along_x(1, [sent[2]])
+    (held,) = run(2, True, (), (), [crossed[0]])
+    held = [held, *run(3, True, (), (), [sent[2]])]
+    along_x(1, [sent[3]])
     along_z(0, [crossed[1]])
-    held = [held, *run(3, True, False, (), [last[0]])]
-    run(3, False, True, held, [sent[3]])
+    run(3, False, (0,), held, [last[0]])
     along_x(2)
-    along_z(1, [crossed[2]])
+    run(3, False, (1,), held, [crossed[2]])
+    along_z(1, [keep[3]])
     along_x(3, [crossed[2]])
     along_z(2, [crossed[3]])
     along_z(3, [last[2]])

time: 104 us -> 107 us (1.029)
  the two profiles are of different devices: /device:TPU:26 before, /device:TPU:2 now
where the time goes in v3:
time: 107 us; the launch traced here: 106 us
  Pallas kernels  62 us (58%)
  starting transfers between devices  24 us (22%)
  waiting for transfers between devices  14.7 us (14%)
  other arithmetic  3.81 us (4%)
    pallas_call x6, Pallas kernels, partial_sums(): pl.pallas_call(functools.partial(kernel, chunk, attends, rows, keeps, len...  62 us
    ppermute x12, starting transfers between devices, swap(): return lax.ppermute(x, ('dp', 'tp'), pairs)  24 us
    ppermute x12, waiting for transfers between devices, swap(): return lax.ppermute(x, ('dp', 'tp'), pairs)  14.7 us
  transfers between devices with their start and end apart: 12, of which 4 were waited for; matrix products, arithmetic and copies ran while one was open for 3% of the time, Pallas kernels for 45%

profile of v3, /device:TPU:2, one launch (start us, length us, event | category | flops | bytes accessed | tf_op | source)
XLA Modules:
  0.0 106.4 jit_solution(1499382171220851786)
XLA Ops:
  0.7 13.8 %chunk0.1 = (bf16[4,128,1024]{2,1,0:T(8,128)(2,1)}, bf16[128,1024]{1,0:T(8,128)(2,1)}) custom-call(s32[1]{0:T(128)S(6)} %copy.10.refs_0_, s32[1,16]{1,0:T(1,128)} %refs_1_.7, f32[32]{0:T(128)} %refs_2_.7, f32[32]{0:T(128)} %refs_3_.7, f32[8,32]{1,0:T(8,128)} %bitcast.13, f32[1,32]{1,0:T(1,128)} %bitcast.21, f32[1,32]{1,0:T(1,128)} %bitcast.25, ...), custom_call_target="tpu_custom_call" | custom-call | flops 10000000000 | bytes 12582912 | tf_op jit(solution)/shard_map/chunk0/pallas_call | solution.py:282
  14.5 2.0 %collective-permute-start = (bf16[4,128,1024]{2,1,0:T(8,128)(2,1)}, bf16[4,128,1024]{2,1,0:T(8,128)(2,1)S(1)}, u32[]{:S(2)}, u32[]{:S(2)}) collective-permute-start(bf16[4,128,1024]{2,1,0:T(8,128)(2,1)} %get-tuple-element.28.refs_12_), channel_id=1, source_target_pairs={{0,1},{1,0},{2,3},{3,2},{4,5},{5,4},{6,7},{7,6},{8,11},{9,10},{10,... | collective-permute-start | bytes 3145736 | tf_op jit(solution)/shard_map/ppermute | solution.py:326
  16.6 0.9 copy-done.7
  17.5 15.2 %chunk1.1 = (bf16[4,128,1024]{2,1,0:T(8,128)(2,1)S(1)}, bf16[2,128,1024]{2,1,0:T(8,128)(2,1)S(1)}, bf16[2,128,1024]{2,1,0:T(8,128)(2,1)S(1)}, bf16[2,128,1024]{2,1,0:T(8,128)(2,1)S(1)}, bf16[2,128,1024]{2,1,0:T(8,128)(2,1)S(1)}) custom-call(s32[1]{0:T(128)S(6)} %copy.10.refs_0_, s32[1,16]{1,0:T(1,128)S(1)} %copy-done.4, f32[32]{0:T(128)S(1)} %copy-done.5, ...), custom_call_target="tpu_custom_call" | custom-call | flops 10000000000 | bytes 20971520 | tf_op jit(solution)/shard_map/chunk1/pallas_call | solution.py:282
  32.8 0.2 collective-permute-start.2
  33.0 0.2 add_convert_fusion.3.refs_11_
  33.2 2.2 %collective-permute-start.1 = (bf16[2,128,1024]{2,1,0:T(8,128)(2,1)S(1)}, bf16[2,128,1024]{2,1,0:T(8,128)(2,1)S(1)}, u32[]{:S(2)}, u32[]{:S(2)}) collective-permute-start(bf16[2,128,1024]{2,1,0:T(8,128)(2,1)S(1)} %add_convert_fusion.3.refs_11_), channel_id=1, source_target_pairs={{0,4},{1,5},{2,6},{3,7},{4,0},{5,1},{6,2},{7,3},{8,12},{9,13},{10,... | collective-permute-start | bytes 1572872 | tf_op jit(solution)/shard_map/ppermute | solution.py:326
  35.4 12.7 %chunk2.1 = (bf16[4,128,1024]{2,1,0:T(8,128)(2,1)S(1)}, bf16[128,1024]{1,0:T(8,128)(2,1)S(1)}) custom-call(s32[1]{0:T(128)S(6)} %copy.10.refs_0_, s32[1,16]{1,0:T(1,128)S(1)} %copy-done.4, f32[32]{0:T(128)S(1)} %copy-done.5, f32[32]{0:T(128)S(1)} %copy-done.6, f32[8,32]{1,0:T(8,128)S(1)} %bitcast.17, f32[1,32]{1,0:T(1,128)S(1)} %bitcast.23, ...), custom_call_target="tpu_custom_call" | custom-call | flops 10000000000 | bytes 12582912 | tf_op jit(solution)/shard_map/chunk2/pallas_call | solution.py:282
  48.1 2.0 %collective-permute-start.5 = (bf16[4,128,1024]{2,1,0:T(8,128)(2,1)S(1)}, bf16[4,128,1024]{2,1,0:T(8,128)(2,1)S(1)}, u32[]{:S(2)}, u32[]{:S(2)}) collective-permute-start(bf16[4,128,1024]{2,1,0:T(8,128)(2,1)S(1)} %get-tuple-element.34.refs_11_), channel_id=1, source_target_pairs={{0,1},{1,0},{2,3},{3,2},{4,5},{5,4},{6,7},{7,6},{8,11},{9,10},{10,... | collective-permute-start | bytes 3145736 | tf_op jit(solution)/shard_map/ppermute | solution.py:326
  50.1 12.6 %chunk3.1 = (bf16[4,128,1024]{2,1,0:T(8,128)(2,1)S(1)}, bf16[128,1024]{1,0:T(8,128)(2,1)S(1)}) custom-call(s32[1]{0:T(128)S(6)} %copy.10.refs_0_, s32[1,16]{1,0:T(1,128)S(1)} %copy-done.4, f32[32]{0:T(128)S(1)} %copy-done.5, f32[32]{0:T(128)S(1)} %copy-done.6, f32[8,32]{1,0:T(8,128)S(1)} %bitcast.19, f32[1,32]{1,0:T(1,128)S(1)} %bitcast.24, ...), custom_call_target="tpu_custom_call" | custom-call | flops 10000000000 | bytes 12582912 | tf_op jit(solution)/shard_map/chunk3/pallas_call | solution.py:282
  62.7 1.0 collective-permute-start.8
  63.7 0.2 add_convert_fusion.2
  63.9 1.5 %collective-permute-start.4 = (bf16[2,128,1024]{2,1,0:T(8,128)(2,1)S(1)}, bf16[2,128,1024]{2,1,0:T(8,128)(2,1)S(1)}, u32[]{:S(2)}, u32[]{:S(2)}) collective-permute-start(bf16[2,128,1024]{2,1,0:T(8,128)(2,1)S(1)} %add_convert_fusion.2), channel_id=1, source_target_pairs={{0,4},{1,5},{2,6},{3,7},{4,0},{5,1},{6,2},{7,3},{8,12},{9,13},{10,... | collective-permute-start | bytes 1572872 | tf_op jit(solution)/shard_map/ppermute | solution.py:326
  65.5 3.3 %collective-permute-start.3 = (bf16[1,128,1024]{2,1,0:T(8,128)(2,1)S(1)}, bf16[1,128,1024]{2,1,0:T(8,128)(2,1)S(1)}, u32[]{:S(2)}, u32[]{:S(2)}) collective-permute-start(bf16[1,128,1024]{2,1,0:T(8,128)(2,1)S(1)} %add_convert_fusion.11.refs_3_), channel_id=1, source_target_pairs={{0,3},{1,2},{2,1},{3,0},{4,7},{5,6},{6,5},{7,4},{8,9},{9,8},{10,11... | collective-permute-start | bytes 786440 | tf_op jit(solution)/shard_map/ppermute | solution.py:326
  68.8 3.8 %half0.1 = (bf16[2,128,1024]{2,1,0:T(8,128)(2,1)S(1)}, bf16[2,128,1024]{2,1,0:T(8,128)(2,1)S(1)}) custom-call(bf16[1024,8192]{1,0:T(8,128)(2,1)} %refs_0_.7, bf16[128,1024]{1,0:T(8,128)(2,1)S(1)} %get-tuple-element.39.refs_1_, bf16[128,1024]{1,0:T(8,128)(2,1)S(1)} %get-tuple-element.40.refs_2_, bf16[1,128,1024]{2,1,0:T(8,128)(2,1)S(1)} %add_convert_fusion.11.refs_3_), custom_call_target="tpu_custom_call" | custom-call | flops 4000000000 | bytes 8388608 | tf_op jit(solution)/shard_map/half0/pallas_call | solution.py:282
  72.7 0.2 add_convert_fusion.1.refs_3_
  72.9 2.2 %collective-permute-start.7 = (bf16[2,128,1024]{2,1,0:T(8,128)(2,1)S(1)}, bf16[2,128,1024]{2,1,0:T(8,128)(2,1)S(1)}, u32[]{:S(2)}, u32[]{:S(2)}) collective-permute-start(bf16[2,128,1024]{2,1,0:T(8,128)(2,1)S(1)} %add_convert_fusion.1.refs_3_), channel_id=1, source_target_pairs={{0,4},{1,5},{2,6},{3,7},{4,0},{5,1},{6,2},{7,3},{8,12},{9,13},{10,... | collective-permute-start | bytes 1572872 | tf_op jit(solution)/shard_map/ppermute | solution.py:326
  75.1 3.8 %half1.1 = (bf16[2,128,1024]{2,1,0:T(8,128)(2,1)S(1)}, bf16[2,128,1024]{2,1,0:T(8,128)(2,1)S(1)}) custom-call(bf16[1024,8192]{1,0:T(8,128)(2,1)} %refs_0_.7, bf16[128,1024]{1,0:T(8,128)(2,1)S(1)} %get-tuple-element.39.refs_1_, bf16[128,1024]{1,0:T(8,128)(2,1)S(1)} %get-tuple-element.40.refs_2_, bf16[2,128,1024]{2,1,0:T(8,128)(2,1)S(1)} %add_convert_fusion.1.refs_3_), custom_call_target="tpu_custom_call" | custom-call | flops 4000000000 | bytes 8388608 | tf_op jit(solution)/shard_map/half1/pallas_call | solution.py:282
  78.9 1.4 %collective-permute-done.4 = bf16[2,128,1024]{2,1,0:T(8,128)(2,1)S(1)} collective-permute-done((bf16[2,128,1024]{2,1,0:T(8,128)(2,1)S(1)}, bf16[2,128,1024]{2,1,0:T(8,128)(2,1)S(1)}, u32[]{:S(2)}, u32[]{:S(2)}) %collective-permute-start.4) | collective-permute-done | bytes 524320 | tf_op jit(solution)/shard_map/ppermute | solution.py:326
  80.4 3.3 %collective-permute-start.6 = (bf16[1,128,1024]{2,1,0:T(8,128)(2,1)S(1)}, bf16[1,128,1024]{2,1,0:T(8,128)(2,1)S(1)}, u32[]{:S(2)}, u32[]{:S(2)}) collective-permute-start(bf16[1,128,1024]{2,1,0:T(8,128)(2,1)S(1)} %add_convert_fusion.9), channel_id=1, source_target_pairs={{0,3},{1,2},{2,1},{3,0},{4,7},{5,6},{6,5},{7,4},{8,9},{9,8},{10,11... | collective-permute-start | bytes 786440 | tf_op jit(solution)/shard_map/ppermute | solution.py:326
  83.8 0.2 add_convert_fusion
  84.0 1.4 %collective-permute-start.10 = (bf16[2,128,1024]{2,1,0:T(8,128)(2,1)S(1)}, bf16[2,128,1024]{2,1,0:T(8,128)(2,1)S(1)}, u32[]{:S(2)}, u32[]{:S(2)}) collective-permute-start(bf16[2,128,1024]{2,1,0:T(8,128)(2,1)S(1)} %add_convert_fusion), channel_id=1, source_target_pairs={{0,4},{1,5},{2,6},{3,7},{4,0},{5,1},{6,2},{7,3},{8,12},{9,13},{10,... | collective-permute-start | bytes 1572872 | tf_op jit(solution)/shard_map/ppermute | solution.py:326
  85.4 0.2 fusion
  85.6 6.0 %collective-permute-done.7 = bf16[2,128,1024]{2,1,0:T(8,128)(2,1)S(1)} collective-permute-done((bf16[2,128,1024]{2,1,0:T(8,128)(2,1)S(1)}, bf16[2,128,1024]{2,1,0:T(8,128)(2,1)S(1)}, u32[]{:S(2)}, u32[]{:S(2)}) %collective-permute-start.7) | collective-permute-done | bytes 524320 | tf_op jit(solution)/shard_map/ppermute | solution.py:326
  91.7 2.7 %collective-permute-start.9 = (bf16[1,128,1024]{2,1,0:T(8,128)(2,1)S(1)}, bf16[1,128,1024]{2,1,0:T(8,128)(2,1)S(1)}, u32[]{:S(2)}, u32[]{:S(2)}) collective-permute-start(bf16[1,128,1024]{2,1,0:T(8,128)(2,1)S(1)} %add_convert_fusion.7), channel_id=1, source_target_pairs={{0,3},{1,2},{2,1},{3,0},{4,7},{5,6},{6,5},{7,4},{8,9},{9,8},{10,11... | collective-permute-start | bytes 786440 | tf_op jit(solution)/shard_map/ppermute | solution.py:326
  94.4 0.2 fusion.1
  94.6 3.1 %collective-permute-done.10 = bf16[2,128,1024]{2,1,0:T(8,128)(2,1)S(1)} collective-permute-done((bf16[2,128,1024]{2,1,0:T(8,128)(2,1)S(1)}, bf16[2,128,1024]{2,1,0:T(8,128)(2,1)S(1)}, u32[]{:S(2)}, u32[]{:S(2)}) %collective-permute-start.10) | collective-permute-done | bytes 524320 | tf_op jit(solution)/shard_map/ppermute | solution.py:326
  97.8 2.2 %collective-permute-start.11 = (bf16[1,128,1024]{2,1,0:T(8,128)(2,1)S(1)}, bf16[1,128,1024]{2,1,0:T(8,128)(2,1)S(1)}, u32[]{:S(2)}, u32[]{:S(2)}) collective-permute-start(bf16[1,128,1024]{2,1,0:T(8,128)(2,1)S(1)} %add_convert_fusion.5), channel_id=1, source_target_pairs={{0,3},{1,2},{2,1},{3,0},{4,7},{5,6},{6,5},{7,4},{8,9},{9,8},{10,11... | collective-permute-start | bytes 786440 | tf_op jit(solution)/shard_map/ppermute | solution.py:326
  100.0 0.2 fusion.2
  100.2 1.2 %maximum_maximum_fusion = bf16[512,1024]{1,0:T(8,128)(2,1)} fusion(bf16[128,1024]{1,0:T(8,128)(2,1)S(1)} %fusion.2, bf16[128,1024]{1,0:T(8,128)(2,1)S(1)} %fusion.1, bf16[128,1024]{1,0:T(8,128)(2,1)S(1)} %fusion, bf16[512]{0:T(512)(128)(2,1)S(1)} %pad.3.clone), kind=kLoop, calls=%fused_computation | loop fusion | flops 4194304 | bytes 1836032 | tf_op jit(solution)/shard_map/concatenate | solution.py:381
  101.4 4.1 %collective-permute-done.11 = bf16[1,128,1024]{2,1,0:T(8,128)(2,1)S(1)} collective-permute-done((bf16[1,128,1024]{2,1,0:T(8,128)(2,1)S(1)}, bf16[1,128,1024]{2,1,0:T(8,128)(2,1)S(1)}, u32[]{:S(2)}, u32[]{:S(2)}) %collective-permute-start.11) | collective-permute-done | bytes 262176 | tf_op jit(solution)/shard_map/ppermute | solution.py:326
  105.5 0.9 fusion.4
  (29 shorter events, 0.5 us)
Async XLA Ops:
  0.7 15.9 %copy-start.3 = (f32[32,8]{0,1:T(8,128)S(1)}, f32[32,8]{0,1:T(8,128)}, u32[]{:S(2)}) copy-start(f32[32,8]{0,1:T(8,128)} %param.14) | copy-start | bytes 3076
  0.7 15.9 %copy-start.4 = (s32[1,16]{1,0:T(1,128)S(1)}, s32[1,16]{1,0:T(1,128)}, u32[]{:S(2)}) copy-start(s32[1,16]{1,0:T(1,128)} %refs_1_.7) | copy-start | bytes 196
  0.7 15.9 %copy-start.5 = (f32[32]{0:T(128)S(1)}, f32[32]{0:T(128)}, u32[]{:S(2)}) copy-start(f32[32]{0:T(128)} %refs_2_.7) | copy-start | bytes 388
  0.7 15.9 %copy-start.6 = (f32[32]{0:T(128)S(1)}, f32[32]{0:T(128)}, u32[]{:S(2)}) copy-start(f32[32]{0:T(128)} %refs_3_.7) | copy-start | bytes 388
  14.5 18.4 %collective-permute-start = (bf16[4,128,1024]{2,1,0:T(8,128)(2,1)}, bf16[4,128,1024]{2,1,0:T(8,128)(2,1)S(1)}, u32[]{:S(2)}, u32[]{:S(2)}) collective-permute-start(bf16[4,128,1024]{2,1,0:T(8,128)(2,1)} %get-tuple-element.28.refs_12_), channel_id=1, source_target_pairs={{0,1},{1,0},{2,3},{3,2},{4,5},{5,4},{6,7},{7,6},{8,11},{9,10},{10,... | collective-permute-start | bytes 3145736 | tf_op jit(solution)/shard_map/ppermute | solution.py:326
  16.6 1.0 copy-start.7
  17.5 17.9 %copy-start = (bf16[512,1024]{1,0:T(8,128)(2,1)S(1)}, bf16[512,1024]{1,0:T(8,128)(2,1)}, u32[]{:S(2)}) copy-start(bf16[512,1024]{1,0:T(8,128)(2,1)} %refs_8_.7) | copy-start | bytes 3145732
  17.5 17.9 %copy-start.1 = (bf16[16,128,256]{2,1,0:T(8,128)(2,1)S(1)}, bf16[16,128,256]{2,1,0:T(8,128)(2,1)}, u32[]{:S(2)}) copy-start(bf16[16,128,256]{2,1,0:T(8,128)(2,1)} %refs_9_.7) | copy-start | bytes 3145732
  32.8 30.9 %collective-permute-start.2 = (bf16[4,128,1024]{2,1,0:T(8,128)(2,1)S(1)}, bf16[4,128,1024]{2,1,0:T(8,128)(2,1)S(1)}, u32[]{:S(2)}, u32[]{:S(2)}) collective-permute-start(bf16[4,128,1024]{2,1,0:T(8,128)(2,1)S(1)} %get-tuple-element.31), channel_id=1, source_target_pairs={{0,1},{1,0},{2,3},{3,2},{4,5},{5,4},{6,7},{7,6},{8,11},{9,10},{10,... | collective-permute-start | bytes 3145736 | tf_op jit(solution)/shard_map/ppermute | solution.py:326
  33.2 32.2 %collective-permute-start.1 = (bf16[2,128,1024]{2,1,0:T(8,128)(2,1)S(1)}, bf16[2,128,1024]{2,1,0:T(8,128)(2,1)S(1)}, u32[]{:S(2)}, u32[]{:S(2)}) collective-permute-start(bf16[2,128,1024]{2,1,0:T(8,128)(2,1)S(1)} %add_convert_fusion.3.refs_11_), channel_id=1, source_target_pairs={{0,4},{1,5},{2,6},{3,7},{4,0},{5,1},{6,2},{7,3},{8,12},{9,13},{10,... | collective-permute-start | bytes 1572872 | tf_op jit(solution)/shard_map/ppermute | solution.py:326
  48.1 2.0 %copy-start.2 = (bf16[4,128,1024]{2,1,0:T(8,128)(2,1)}, bf16[4,128,1024]{2,1,0:T(8,128)(2,1)S(1)}, u32[]{:S(2)}) copy-start(bf16[4,128,1024]{2,1,0:T(8,128)(2,1)S(1)} %get-tuple-element.34.refs_11_) | copy-start | bytes 3145732
  48.1 24.5 %collective-permute-start.5 = (bf16[4,128,1024]{2,1,0:T(8,128)(2,1)S(1)}, bf16[4,128,1024]{2,1,0:T(8,128)(2,1)S(1)}, u32[]{:S(2)}, u32[]{:S(2)}) collective-permute-start(bf16[4,128,1024]{2,1,0:T(8,128)(2,1)S(1)} %get-tuple-element.34.refs_11_), channel_id=1, source_target_pairs={{0,1},{1,0},{2,3},{3,2},{4,5},{5,4},{6,7},{7,6},{8,11},{9,10},{10,... | collective-permute-start | bytes 3145736 | tf_op jit(solution)/shard_map/ppermute | solution.py:326
  62.7 21.1 %collective-permute-start.8 = (bf16[4,128,1024]{2,1,0:T(8,128)(2,1)S(1)}, bf16[4,128,1024]{2,1,0:T(8,128)(2,1)S(1)}, u32[]{:S(2)}, u32[]{:S(2)}) collective-permute-start(bf16[4,128,1024]{2,1,0:T(8,128)(2,1)S(1)} %get-tuple-element.35), channel_id=1, source_target_pairs={{0,1},{1,0},{2,3},{3,2},{4,5},{5,4},{6,7},{7,6},{8,11},{9,10},{10,... | collective-permute-start | bytes 3145736 | tf_op jit(solution)/shard_map/ppermute | solution.py:326
  63.9 16.4 %collective-permute-start.4 = (bf16[2,128,1024]{2,1,0:T(8,128)(2,1)S(1)}, bf16[2,128,1024]{2,1,0:T(8,128)(2,1)S(1)}, u32[]{:S(2)}, u32[]{:S(2)}) collective-permute-start(bf16[2,128,1024]{2,1,0:T(8,128)(2,1)S(1)} %add_convert_fusion.2), channel_id=1, source_target_pairs={{0,4},{1,5},{2,6},{3,7},{4,0},{5,1},{6,2},{7,3},{8,12},{9,13},{10,... | collective-permute-start | bytes 1572872 | tf_op jit(solution)/shard_map/ppermute | solution.py:326
  65.5 19.9 %collective-permute-start.3 = (bf16[1,128,1024]{2,1,0:T(8,128)(2,1)S(1)}, bf16[1,128,1024]{2,1,0:T(8,128)(2,1)S(1)}, u32[]{:S(2)}, u32[]{:S(2)}) collective-permute-start(bf16[1,128,1024]{2,1,0:T(8,128)(2,1)S(1)} %add_convert_fusion.11.refs_3_), channel_id=1, source_target_pairs={{0,3},{1,2},{2,1},{3,0},{4,7},{5,6},{6,5},{7,4},{8,9},{9,8},{10,11... | collective-permute-start | bytes 786440 | tf_op jit(solution)/shard_map/ppermute | solution.py:326
  72.9 18.7 %collective-permute-start.7 = (bf16[2,128,1024]{2,1,0:T(8,128)(2,1)S(1)}, bf16[2,128,1024]{2,1,0:T(8,128)(2,1)S(1)}, u32[]{:S(2)}, u32[]{:S(2)}) collective-permute-start(bf16[2,128,1024]{2,1,0:T(8,128)(2,1)S(1)} %add_convert_fusion.1.refs_3_), channel_id=1, source_target_pairs={{0,4},{1,5},{2,6},{3,7},{4,0},{5,1},{6,2},{7,3},{8,12},{9,13},{10,... | collective-permute-start | bytes 1572872 | tf_op jit(solution)/shard_map/ppermute | solution.py:326
  80.4 14.0 %collective-permute-start.6 = (bf16[1,128,1024]{2,1,0:T(8,128)(2,1)S(1)}, bf16[1,128,1024]{2,1,0:T(8,128)(2,1)S(1)}, u32[]{:S(2)}, u32[]{:S(2)}) collective-permute-start(bf16[1,128,1024]{2,1,0:T(8,128)(2,1)S(1)} %add_convert_fusion.9), channel_id=1, source_target_pairs={{0,3},{1,2},{2,1},{3,0},{4,7},{5,6},{6,5},{7,4},{8,9},{9,8},{10,11... | collective-permute-start | bytes 786440 | tf_op jit(solution)/shard_map/ppermute | solution.py:326
  84.0 13.7 %collective-permute-start.10 = (bf16[2,128,1024]{2,1,0:T(8,128)(2,1)S(1)}, bf16[2,128,1024]{2,1,0:T(8,128)(2,1)S(1)}, u32[]{:S(2)}, u32[]{:S(2)}) collective-permute-start(bf16[2,128,1024]{2,1,0:T(8,128)(2,1)S(1)} %add_convert_fusion), channel_id=1, source_target_pairs={{0,4},{1,5},{2,6},{3,7},{4,0},{5,1},{6,2},{7,3},{8,12},{9,13},{10,... | collective-permute-start | bytes 1572872 | tf_op jit(solution)/shard_map/ppermute | solution.py:326
  91.7 8.3 %collective-permute-start.9 = (bf16[1,128,1024]{2,1,0:T(8,128)(2,1)S(1)}, bf16[1,128,1024]{2,1,0:T(8,128)(2,1)S(1)}, u32[]{:S(2)}, u32[]{:S(2)}) collective-permute-start(bf16[1,128,1024]{2,1,0:T(8,128)(2,1)S(1)} %add_convert_fusion.7), channel_id=1, source_target_pairs={{0,3},{1,2},{2,1},{3,0},{4,7},{5,6},{6,5},{7,4},{8,9},{9,8},{10,11... | collective-permute-start | bytes 786440 | tf_op jit(solution)/shard_map/ppermute | solution.py:326
  97.8 7.7 %collective-permute-start.11 = (bf16[1,128,1024]{2,1,0:T(8,128)(2,1)S(1)}, bf16[1,128,1024]{2,1,0:T(8,128)(2,1)S(1)}, u32[]{:S(2)}, u32[]{:S(2)}) collective-permute-start(bf16[1,128,1024]{2,1,0:T(8,128)(2,1)S(1)} %add_convert_fusion.5), channel_id=1, source_target_pairs={{0,3},{1,2},{2,1},{3,0},{4,7},{5,6},{6,5},{7,4},{8,9},{9,8},{10,11... | collective-permute-start | bytes 786440 | tf_op jit(solution)/shard_map/ppermute | solution.py:326
